TPU v7x, 128 devices: a whole 4x4x4 slice. The times are simulated.
128 devices in a mesh: dp: 32 (over y, x, core), tensor: 4 (over z).
Axes of the slice: x: 4, y: 4, z: 4, core: 2. Of those that a mesh axis runs over, the one named last changes fastest.
Arguments:
- attn_heads: bfloat16 [1024, 3584], P('dp', 'tensor'), may hold values from -6 to 6
- out_weight: bfloat16 [3584, 3584], P('tensor'), may hold values from -0.09375 to 0.09375
- residual: bfloat16 [1024, 3584], P(('dp', 'tensor')), may hold values from -6 to 6
- norm_gain: bfloat16 [3584], replicated, may hold values from 0.099609375 to 1.8984375
- shared_gate: bfloat16 [3584], replicated, may hold values from -0.09375 to 0.09375
- shared_gate_proj: bfloat16 [3584, 20480], P(None, ('dp', 'tensor')), may hold values from -0.09375 to 0.09375
- shared_up_proj: bfloat16 [3584, 20480], P(None, ('dp', 'tensor')), may hold values from -0.09375 to 0.09375
- shared_down_proj: bfloat16 [20480, 3584], P(('dp', 'tensor')), may hold values from -0.0390625 to 0.0390625
- expert_gate: bfloat16 [128, 3584, 640], P(('dp', 'tensor')), may hold values from -0.09375 to 0.09375
- expert_up_weight: bfloat16 [128, 3584, 640], P(('dp', 'tensor')), may hold values from -0.09375 to 0.09375
- expert_down: bfloat16 [128, 640, 3584], P(('dp', 'tensor')), may hold values from -0.15625 to 0.15625
- expert_choice: int32 [1024, 8], P(('dp', 'tensor')), may hold values from 0 to 63, all different within a row; in each aligned block of 8 rows (0 to 7, 8 to 15, ...) at most 2 rows name the same one
- gate_probs: float32 [1024, 8], P(('dp', 'tensor')), may hold values from 0.02 to 0.4
Outputs:
- mid: bfloat16 [1024, 3584], P(('dp', 'tensor'))
- ffn_out: bfloat16 [1024, 3584], P(('dp', 'tensor'))
Inputs may be any that keep to these rules, and one draw needn't show every extreme that they name: `expert_choice`: the 8 experts of a token differ. Among the 8 rows of one device (aligned blocks) no expert is named more than 2 times, and in every draw some expert is named exactly 2 times in some block.
All inputs are finite; a program needn't handle non-finite values.
Results may differ from a plain program's by a relative error of at most 0.014.
Values may be sent and summed in bfloat16 or wider, within the bound.
A program may use at most 128 MiB of HBM per device.

v0:
```python
import jax
import jax.numpy as jnp
from jax import lax
from jax.sharding import PartitionSpec as P


def on_device(
    attn_heads,
    out_weight,
    residual,
    norm_gain,
    shared_gate,
    shared_gate_proj,
    shared_up_proj,
    shared_down_proj,
    expert_gate,
    expert_up_weight,
    expert_down,
    expert_choice,
    gate_probs,
):
    tok_rows = residual.shape[0]
    width = residual.shape[1]
    top_count = expert_choice.shape[1]
    devices_all = lax.axis_size("dp") * lax.axis_size("tensor")
    experts_all = devices_all // 2
    capacity = tok_rows * top_count * 2 // experts_all
    block = attn_heads
    projected = lax.psum_scatter(
        jnp.dot(block, out_weight, preferred_element_type=jnp.float32),
        "tensor",
        scatter_dimension=0,
        tiled=True,
    )
    mid = (residual.astype(jnp.float32) + projected).astype(jnp.bfloat16)
    midf = mid.astype(jnp.float32)
    scale = lax.rsqrt(jnp.mean(midf * midf, axis=1, keepdims=True) + 1e-06)
    normed = (midf * scale * norm_gain.astype(jnp.float32)).astype(jnp.bfloat16)
    share = jax.nn.sigmoid(jnp.dot(normed, shared_gate, preferred_element_type=jnp.float32))
    piece = lax.all_gather(normed, ("dp", "tensor"), axis=0, tiled=True)
    gate = jnp.dot(piece, shared_gate_proj, preferred_element_type=jnp.float32)
    upper = jnp.dot(piece, shared_up_proj, preferred_element_type=jnp.float32)
    hidden_all = (jax.nn.silu(gate) * upper).astype(jnp.bfloat16)
    expert_ids = lax.broadcasted_iota(jnp.int32, (1, 1, experts_all), 2)
    picked = (expert_choice[:, :, None] == expert_ids).astype(jnp.int32)
    per_expert = jnp.sum(picked, axis=1)
    earlier = jnp.cumsum(per_expert, axis=0) - per_expert
    slot = jnp.sum(picked * earlier[:, None, :], axis=2)
    slot_ids = lax.broadcasted_iota(jnp.int32, (1, 1, capacity), 2)
    at_slot = (slot[:, :, None] == slot_ids).astype(jnp.float32)
    picked_float = picked.astype(jnp.float32)
    place = (
        jnp.einsum("tke,tkc->ect", picked_float, at_slot)
        .reshape(experts_all * capacity, tok_rows)
        .astype(jnp.bfloat16)
    )
    outgoing = jnp.dot(place, normed, preferred_element_type=jnp.float32).astype(jnp.bfloat16)
    outgoing = jnp.concatenate([outgoing, outgoing], axis=0).reshape(devices_all, capacity, width)
    weigh = jnp.einsum("tke,tkc,tk->tec", picked_float, at_slot, gate_probs).reshape(
        tok_rows, experts_all * capacity
    )
    received = lax.all_to_all(outgoing, ("dp", "tensor"), split_axis=0, concat_axis=0, tiled=True)
    layout = received.shape
    token_row_block = received.reshape(-1, width)
    expert_gate_value = jnp.dot(token_row_block, expert_gate[0], preferred_element_type=jnp.float32)
    expert_up_value = jnp.dot(
        token_row_block, expert_up_weight[0], preferred_element_type=jnp.float32
    )
    expert_hidden_state = (jax.nn.silu(expert_gate_value) * expert_up_value).astype(jnp.bfloat16)
    result = jnp.dot(
        expert_hidden_state, expert_down[0], preferred_element_type=jnp.float32
    ).astype(jnp.bfloat16)
    expert_out = result.reshape(layout)
    block = hidden_all
    shared_out = lax.psum_scatter(
        jnp.dot(block, shared_down_proj, preferred_element_type=jnp.float32),
        ("dp", "tensor"),
        scatter_dimension=0,
        tiled=True,
    )
    halves = lax.all_to_all(
        expert_out, ("dp", "tensor"), split_axis=0, concat_axis=0, tiled=True
    ).astype(jnp.float32)
    summed = (halves[:experts_all] + halves[experts_all:]).reshape(experts_all * capacity, width)
    routed = jnp.dot(
        weigh, summed, precision=lax.Precision.HIGHEST, preferred_element_type=jnp.float32
    )
    ffn_out = (share[:, None] * shared_out + routed).astype(jnp.bfloat16)
    return (mid, ffn_out)


def solution(mesh):
    in_specs = (
        P("dp", "tensor"),
        P("tensor", None),
        P(("dp", "tensor"), None),
        P(),
        P(),
        P(None, ("dp", "tensor")),
        P(None, ("dp", "tensor")),
        P(("dp", "tensor"), None),
        P(("dp", "tensor"), None, None),
        P(("dp", "tensor"), None, None),
        P(("dp", "tensor"), None, None),
        P(("dp", "tensor"), None),
        P(("dp", "tensor"), None),
    )
    out_specs = (P(("dp", "tensor"), None), P(("dp", "tensor"), None))
    return jax.shard_map(
        on_device, mesh=mesh, in_specs=in_specs, out_specs=out_specs, check_vma=False
    )
```

profile of v0, /device:TPU:1, one launch (start us, length us, event | category | flops | bytes accessed | tf_op | source)
XLA Modules:
  0.0 811.7 jit_solution(14572011557552839854)
XLA Ops:
  7.2 0.0 copy-start
  7.2 0.0 copy-start.7
  7.2 0.0 copy-start.5
  7.2 0.0 reduce-scatter.3.cloned.1.call-start
  7.2 4.9 fusion.45
  12.2 0.0 reduce-scatter.3.cloned.1.call-update
  12.2 0.0 all-gather.2.cloned.1.call-start
  12.2 0.0 copy-done.7
  12.3 23.0 %reduce-scatter.3.cloned.1.call-done = f32[8,3584]{1,0:T(8,128)} async-done(((f32[32,3584]{1,0:T(8,128)}), f32[8,3584]{1,0:T(8,128)}) %reduce-scatter.3.cloned.1.call-update) | async-done | bytes 114704 | tf_op jit(solution)/shard_map/reduce_scatter | solution.py:29
  35.3 0.0 copy-done.5
  35.3 1.0 fusion.30
  36.3 0.0 copy-start.4
  36.3 0.7 fusion.32
  37.1 0.0 all-gather.2.cloned.1.call-update
  37.1 0.0 copy-start.2
  37.1 0.0 reduce-scatter.5.cloned.1.call-start
  37.1 73.0 %all-gather.2.cloned.1.call-done = bf16[1024,3584]{1,0:T(8,128)(2,1)} async-done(((bf16[8,3584]{1,0:T(8,128)(2,1)}), bf16[1024,3584]{1,0:T(8,128)(2,1)}) %all-gather.2.cloned.1.call-update) | async-done | bytes 7340048 | tf_op jit(solution)/shard_map/all_gather | solution.py:40
  110.2 5.9 fusion.46
  116.0 0.0 copy-done.4
  116.0 0.0 copy-done
  116.0 0.0 copy-done.2
  116.0 12.8 %fusion.12 = f32[1024,3584]{1,0:T(8,128)} fusion(bf16[160,3584]{1,0:T(8,128)(2,1)S(1)} %copy-done, bf16[1024,3584]{1,0:T(8,128)(2,1)} %all-gather.2.cloned.1.call-done, bf16[3584,160]{0,1:T(8,128)(2,1)S(1)} %copy-done.2, f32[1024,160]{0,1:T(8,128)S(1)} %fusion.46), kind=kOutput, calls=%fused_computation.16 | convolution fusion | flops 2349793280 | bytes 24969216 | tf_op jit(solution)/shard_map/dot_general | solution.py:76
  128.9 0.0 copy-start.6
  128.9 0.0 copy-start.3
  128.9 0.0 reduce-scatter.5.cloned.1.call-update
  128.9 0.7 copy-done.6
  129.5 0.1 convert_reduce_fusion
  129.7 0.3 select_reduce_fusion
  129.9 0.2 fusion.16
  130.1 0.1 copy.18
  130.3 0.0 copy-done.3
  130.3 0.4 convolution_convert_fusion.1
  130.6 1.4 pad_maximum_fusion
  132.0 3.9 reshape.38
  135.9 33.0 %all_to_all.10 = bf16[128,2,3584]{2,1,0:T(2,128)(2,1)} all-to-all(bf16[128,2,3584]{2,1,0:T(2,128)(2,1)S(1)} %reshape.38), channel_id=1, replica_groups=mesh['dp'=32,'tensor'=4] {'dp','tensor'}, dimensions={0} | all-to-all | bytes 3670016 | tf_op jit(solution)/shard_map/all_to_all | solution.py:62
  168.9 4.1 reshape.39
  172.9 3.9 fusion.3
  176.9 8.0 convolution_convert_fusion
  184.9 4.8 reshape.40
  189.6 0.0 copy-start.8
  189.6 0.0 copy-start.9
  189.6 4.5 all-to-all-start.1
  194.1 0.0 copy-done.8
  194.2 0.0 copy-done.9
  194.2 0.2 fusion.33
  194.4 0.1 fusion.20
  194.5 27.4 %all-to-all-done.1 = bf16[128,2,3584]{2,1,0:T(2,128)(2,1)S(1)} async-done(((bf16[128,2,3584]{2,1,0:T(2,128)(2,1)}), bf16[128,2,3584]{2,1,0:T(2,128)(2,1)S(1)}, u32[]{:S(2)}, u32[]{:S(2)}) %all-to-all-start.1) | async-done | bytes 1835040 | tf_op jit(solution)/shard_map/all_to_all | solution.py:81
  221.9 1.3 convert_element_type.63
  223.2 0.0 copy-start.1
  223.2 0.9 slice_add_fusion
  224.2 578.3 %reduce-scatter.5.cloned.1.call-done = f32[8,3584]{1,0:T(8,128)} async-done(((f32[1024,3584]{1,0:T(8,128)}), f32[8,3584]{1,0:T(8,128)}) %reduce-scatter.5.cloned.1.call-update) | async-done | bytes 114704 | tf_op jit(solution)/shard_map/reduce_scatter | solution.py:75
  802.4 2.7 fusion.6
  805.1 0.0 copy-done.1
  (5 shorter events, 0.1 us)
Async XLA Ops:
  7.2 108.9 %copy-start = (bf16[160,3584]{1,0:T(8,128)(2,1)S(1)}, bf16[160,3584]{1,0:T(8,128)(2,1)}, u32[]{:S(2)}) copy-start(bf16[160,3584]{1,0:T(8,128)(2,1)} %param.20) | copy-start | bytes 3440644
  7.2 5.1 copy-start.7
  7.2 28.1 %copy-start.5 = (bf16[8,3584]{1,0:T(8,128)(2,1)S(1)}, bf16[8,3584]{1,0:T(8,128)(2,1)}, u32[]{:S(2)}) copy-start(bf16[8,3584]{1,0:T(8,128)(2,1)} %param.15) | copy-start | bytes 172036
  7.2 28.1 %reduce-scatter.3.cloned.1.call-start = ((), (), s32[]{:S(2)}) async-start(), calls=%async_computation.4 | async-start | bytes 573440 | tf_op jit(solution)/shard_map/reduce_scatter | solution.py:29
  12.2 98.0 %all-gather.2.cloned.1.call-start = ((), (), s32[]{:S(2)}) async-start(), calls=%async_computation.5 | async-start | bytes 7397376 | tf_op jit(solution)/shard_map/all_gather | solution.py:40
  36.3 79.7 %copy-start.4 = (bf16[8,3584]{1,0:T(8,128)(2,1)}, bf16[8,3584]{1,0:T(8,128)(2,1)S(1)}, u32[]{:S(2)}) copy-start(bf16[8,3584]{1,0:T(8,128)(2,1)S(1)} %get-tuple-element.3) | copy-start | bytes 172036
  37.1 79.0 %copy-start.2 = (bf16[3584,160]{0,1:T(8,128)(2,1)S(1)}, bf16[3584,160]{0,1:T(8,128)(2,1)}, u32[]{:S(2)}) copy-start(bf16[3584,160]{0,1:T(8,128)(2,1)} %param.19) | copy-start | bytes 3440644
  37.1 765.3 %reduce-scatter.5.cloned.1.call-start = ((), (), s32[]{:S(2)}) async-start(), calls=%async_computation.6 | async-start | bytes 14794752 | tf_op jit(solution)/shard_map/reduce_scatter | solution.py:75
  128.9 0.7 copy-start.6
  128.9 1.4 copy-start.3
  189.6 4.5 copy-start.8
  189.6 4.5 copy-start.9
  189.6 32.3 %all-to-all-start.1 = ((bf16[128,2,3584]{2,1,0:T(2,128)(2,1)}), bf16[128,2,3584]{2,1,0:T(2,128)(2,1)S(1)}, u32[]{:S(2)}, u32[]{:S(2)}) async-start(bf16[128,2,3584]{2,1,0:T(2,128)(2,1)} %reshape.40), calls=%async_computation.3 | async-start | bytes 3670016 | tf_op jit(solution)/shard_map/all_to_all | solution.py:81
  223.2 581.9 %copy-start.1 = (bf16[160,3584]{1,0:T(8,128)(2,1)S(1)}, bf16[160,3584]{1,0:T(8,128)(2,1)}, u32[]{:S(2)}) copy-start(bf16[160,3584]{1,0:T(8,128)(2,1)} %param.20) | copy-start | bytes 3440644
Sparse Core Ops, SparseCore 0:
  12.3 22.9 reduce-scatter.2
  39.3 70.8 all-gather.1
  129.0 673.3 reduce-scatter.4
where the time goes:
time: 820 us; the launch traced here: 812 us
  waiting for transfers between devices  702 us (86%)
  matrix products  39.1 us (5%)
  blocking collectives  33 us (4%)
  between operations  13.9 us (2%)
  local copies, waits for them, and re-layouts  13.5 us (2%)
    reduce_scatter x1, waiting for transfers between devices, on_device(): lax.psum_scatter(jnp.dot(block, shared_down_proj, preferred_element_type=...  578 us
    all_gather x1, waiting for transfers between devices, on_device(): piece = lax.all_gather(normed, ('dp', 'tensor'), axis=0, tiled=True)  73 us
    all_to_all x1, blocking collectives, on_device(): lax.all_to_all(outgoing, ('dp', 'tensor'), split_axis=0, concat_axis=0, t...  33 us
    all_to_all x1, waiting for transfers between devices, on_device(): lax.all_to_all(expert_out, ('dp', 'tensor'), split_axis=0, concat_axis=0,...  27.4 us
    reduce_scatter x1, waiting for transfers between devices, on_device(): lax.psum_scatter(jnp.dot(block, out_weight, preferred_element_type=jnp.fl...  23 us
  transfers between devices with their start and end apart: 4, of which 4 were waited for; matrix products, arithmetic and copies ran while one was open for 4% of the time, Pallas kernels for 0%

commit v1 on v0

v1 whole, which is shorter than its diff:
```python
import jax
import jax.numpy as jnp
from jax import lax
from jax.experimental import pallas as pl
from jax.experimental.pallas import tpu as pltpu
from jax.sharding import PartitionSpec as P

MESH = pl.DeviceIdType.MESH
BF = jnp.bfloat16
F32 = jnp.float32
TOK = 8
PAIR = 16
D = 3584
HALF_D = D // 2
WIDTHS = (640, 640, 512)
OFFS = (0, 640, 1280)
CARRY = 640
ORDERS = ((2, 1, 0), (1, 0, 2), (0, 2, 1))
HID = 160
HALF = 640
EXPERTS = 64
CHUNK = 256
SLOTS = 64
N_AG = 3 * (3 + 4 + 6 + 7)
N_RS = 3 * (1 + 6 + 6 + 3)


def silu(v):
    return v / (1.0 + jnp.exp(-v))


def kernel(
    heads, out_w, residual, gain, sgate, sgp, sup, sdn, eg, eu, ed, choice, probs,
    mid_out, ffn_out,
    wo, wsg, wsu, weg, weu, wed, rhs,
    part, sbuf, rz, nx, rx, g,
    place, pslot, share_s, lhs, xe, he,
    s0, s1, s2, t0, t1, t2, u0, u1, u2,
    a0, a1, a2, b0, b1, b2, c0, c1, c2,
    fin, rfin,
    wo_sem, w_sem, zs_sem, zr_sem, x_sem, ags, agr, rss, rsr,
):
    dp = lax.axis_index("dp")
    z0 = lax.axis_index("tensor")
    core = lax.rem(dp, 2)
    other = 1 - core
    pos = (dp // 8, lax.rem(dp // 2, 4), z0)

    def device(y, x, c, z):
        return ((y * 4 + x) * 2 + c, z)

    def near(axis, k):
        return lax.rem(pos[axis] + k, 4)

    def peer(axis, k):
        at = list(pos)
        at[axis] = near(axis, k)
        return device(at[0], at[1], core, at[2])

    sibling = device(pos[0], pos[1], other, pos[2])

    barrier = pltpu.get_barrier_semaphore()
    for axis in range(3):
        for k in range(1, 4):
            pl.semaphore_signal(barrier, inc=1, device_id=peer(axis, k), device_id_type=MESH)
    pl.semaphore_signal(barrier, inc=1, device_id=sibling, device_id_type=MESH)

    def wo_copy(j):
        return pltpu.make_async_copy(
            out_w.at[:, pl.ds(pl.multiple_of(j * 256, 256), 256)], wo.at[j], wo_sem.at[j]
        )

    for j in range(7):
        wo_copy(j).start()
        wo_copy(j + 7).start()
    loads = [
        pltpu.make_async_copy(sgp, wsg, w_sem.at[0]),
        pltpu.make_async_copy(sup, wsu, w_sem.at[1]),
        pltpu.make_async_copy(eg.at[0], weg, w_sem.at[2]),
        pltpu.make_async_copy(eu.at[0], weu, w_sem.at[3]),
        pltpu.make_async_copy(ed.at[0], wed, w_sem.at[4]),
    ]
    for h in range(2):
        for y in range(4):
            loads.append(
                pltpu.make_async_copy(
                    sdn.at[:, pl.ds(h * HALF_D, HALF_D)],
                    rhs.at[h, y, pl.ds(0, HID)],
                    w_sem.at[5 + h * 4 + y],
                )
            )
    for load in loads:
        load.start()

    def project(j, carry):
        wo_copy(j).wait()
        wo_copy(j + 7).wait()
        cols = pl.ds(pl.multiple_of(j * 256, 256), 256)
        left = jnp.dot(heads[...], wo[j], preferred_element_type=F32)
        right = jnp.dot(heads[...], wo[j + 7], preferred_element_type=F32)
        part[0, :, :, cols] = left.reshape(4, TOK, 256)
        part[1, :, :, cols] = right.reshape(4, TOK, 256)
        for q in range(4):
            rows = slice(q * TOK, (q + 1) * TOK)
            sbuf[q, :, cols] = jnp.concatenate([left[rows], right[rows]], axis=0).astype(BF)
        return carry

    lax.fori_loop(0, 7, project, 0)

    pl.semaphore_wait(barrier, 10)

    zc = []
    for k in range(1, 4):
        c = pltpu.make_async_remote_copy(
            src_ref=sbuf.at[near(2, k)], dst_ref=rz.at[k - 1],
            send_sem=zs_sem.at[k - 1], recv_sem=zr_sem.at[k - 1],
            device_id=peer(2, k), device_id_type=MESH,
        )
        c.start()
        zc.append(c)

    rhs[:, :, HID:256, :] = jnp.zeros((2, 4, 256 - HID, HALF_D), BF)

    for c in zc:
        c.wait_recv()

    square = jnp.zeros((TOK, 1), F32)
    mids = []
    for h in range(2):
        cols = slice(h * HALF_D, (h + 1) * HALF_D)
        total = part[h, z0]
        for k in range(3):
            total = total + rz[k].astype(F32)[h * TOK : (h + 1) * TOK]
        mid = (residual[:, cols].astype(F32) + total).astype(BF)
        mid_out[:, cols] = mid
        midf = mid.astype(F32)
        mids.append(midf)
        square = square + jnp.sum(midf * midf, axis=1, keepdims=True)
    scale = lax.rsqrt(square * (1.0 / D) + 1e-06)
    logit = jnp.zeros((TOK, 1), F32)
    for h in range(2):
        cols = slice(h * HALF_D, (h + 1) * HALF_D)
        normed = (mids[h] * scale * gain[:, cols].astype(F32)).astype(BF).astype(F32)
        nx[h, :, 0:HALF_D] = normed
        logit = logit + jnp.sum(normed * sgate[:, cols].astype(F32), axis=1, keepdims=True)
    share = 1.0 / (1.0 + jnp.exp(-logit))

    lane = lax.broadcasted_iota(jnp.int32, (TOK, 128), 1)
    facts = jnp.zeros((TOK, 128), F32)
    chosen = choice[...].astype(F32)
    weight = probs[...]
    high = weight.astype(BF).astype(F32)
    low = weight - high
    for k in range(8):
        facts = jnp.where(lane == k, chosen[:, k : k + 1], facts)
        facts = jnp.where(lane == 8 + k, high[:, k : k + 1], facts)
        facts = jnp.where(lane == 16 + k, low[:, k : k + 1], facts)
    share_high = share.astype(BF).astype(F32)
    facts = jnp.where(lane == 24, share_high, facts)
    facts = jnp.where(lane == 25, share - share_high, facts)
    for h in range(2):
        nx[h, :, HALF_D : HALF_D + 128] = facts

    swap = pltpu.make_async_remote_copy(
        src_ref=nx.at[other], dst_ref=rx, send_sem=x_sem.at[0], recv_sem=x_sem.at[1],
        device_id=sibling, device_id_type=MESH,
    )
    swap.start()
    swap.wait_recv()
    mine = nx[core]
    theirs = rx[...]
    first = core == 0
    block = jnp.concatenate(
        [jnp.where(first, mine, theirs), jnp.where(first, theirs, mine)], axis=0
    ).astype(BF)
    for o in range(3):
        g[core, o, pos[0], pos[1], pos[2]] = block[:, o * CARRY : (o + 1) * CARRY]

    pending = []
    count = [0]

    def gsend(o, at, dev):
        i = count[0]
        count[0] += 1
        ref = g.at[(core, o) + tuple(at)]
        c = pltpu.make_async_remote_copy(
            src_ref=ref, dst_ref=ref, send_sem=ags.at[i], recv_sem=agr.at[i],
            device_id=dev, device_id_type=MESH,
        )
        c.start()
        pending.append(c)
        return c

    def where_(o, first_, second, third):
        at = [None, None, None]
        for axis, v in zip(ORDERS[o], (first_, second, third)):
            at[axis] = v
        return at

    ALL, A, B = pl.ds(0, 4), pl.ds(0, 2), pl.ds(2, 2)
    own = [[pos[axis] for axis in ORDERS[o]] for o in range(3)]

    got = [[gsend(o, pos, peer(ORDERS[o][0], k)) for k in range(1, 4)] for o in range(3)]
    stage = []
    for o in range(3):
        for c in got[o]:
            c.wait_recv()
        mine_at = where_(o, ALL, own[o][1], own[o][2])
        ax = ORDERS[o][1]
        stage.append((gsend(o, mine_at, peer(ax, 1)), gsend(o, mine_at, peer(ax, 3))))
    hop = []
    for o in range(3):
        ax = ORDERS[o][1]
        stage[o][0].wait_recv()
        f1 = gsend(o, where_(o, A, near(ax, 3), own[o][2]), peer(ax, 1))
        stage[o][1].wait_recv()
        f2 = gsend(o, where_(o, B, near(ax, 1), own[o][2]), peer(ax, 3))
        hop.append((f1, f2))
    stage = []
    sib = []
    for o in range(3):
        for c in hop[o]:
            c.wait_recv()
        ax = ORDERS[o][2]
        at_a = where_(o, A, ALL, own[o][2])
        at_b = where_(o, B, ALL, own[o][2])
        ra = gsend(o, at_a, peer(ax, 1))
        lb = gsend(o, at_b, peer(ax, 3))
        rb = gsend(o, at_b, peer(ax, 1))
        la = gsend(o, at_a, peer(ax, 3))
        stage.append((ra, lb, rb, la))
        sib.append(gsend(o, where_(o, ALL, ALL, own[o][2]), sibling))
    hop = [[], [], []]
    for event in range(4):
        for o in range(3):
            ax = ORDERS[o][2]
            half = (A, B, B, A)[event]
            came = near(ax, (3, 1, 3, 1)[event])
            at = where_(o, half, ALL, came)
            stage[o][event].wait_recv()
            if event < 2:
                hop[o].append(gsend(o, at, peer(ax, (1, 3)[event])))
            sib.append(gsend(o, at, sibling))
    for event in range(2):
        for o in range(3):
            ax = ORDERS[o][2]
            hop[o][event].wait_recv()
            sib.append(gsend(o, where_(o, (A, B)[event], ALL, near(ax, 2)), sibling))
    for c in sib:
        c.wait_recv()

    expert = lax.rem(dp * 4 + z0, EXPERTS).astype(F32)
    told = g[0, 2, :, :, :, :, 512:640].reshape(1024, 128).astype(F32)
    share_s[...] = jnp.broadcast_to(told[:, 24:25] + told[:, 25:26], (1024, 128))
    turned = told.T
    hit8 = turned[0:8] == expert
    p_row = jnp.sum(jnp.where(hit8, turned[8:16] + turned[16:24], 0.0), axis=0, keepdims=True)
    hit = jnp.sum(jnp.where(hit8, 1.0, 0.0), axis=0, keepdims=True)
    hit = jnp.broadcast_to(hit, (8, 1024))
    token = lax.broadcasted_iota(jnp.int32, (8, 1024), 1)
    rank = jnp.zeros((8, 1024), F32)
    for k in range(1, 8):
        rank = rank + jnp.where(lax.rem(token, 8) >= k, pltpu.roll(hit, k, axis=1), 0.0)
    row = (lax.rem(token // 8, 32) * 2).astype(F32) + rank
    row = jnp.where(hit > 0.5, row, -1000.0)
    row1 = row[0:1]
    column = jnp.broadcast_to(row1, (128, 1024)).T
    lane1 = lax.broadcasted_iota(jnp.int32, (1024, 128), 1).astype(F32)
    lhs[:, :, 0:128] = jnp.zeros((4, CHUNK, 128), BF)
    lhs[:, :, 128:256] = (
        jnp.where(lane1 - (HID - 128.0) == column, 1.0, 0.0).astype(BF).reshape(4, CHUNK, 128)
    )
    slot_id = lax.broadcasted_iota(jnp.int32, (SLOTS, CHUNK), 0).astype(F32)
    for y in range(4):
        cols = slice(y * CHUNK, (y + 1) * CHUNK)
        chosen_y = jnp.where(slot_id == row1[:, cols], 1.0, 0.0)
        place[y] = chosen_y.astype(BF)
        pslot[pl.ds(y * SLOTS, SLOTS)] = jnp.broadcast_to(
            jnp.sum(chosen_y * p_row[:, cols], axis=1, keepdims=True), (SLOTS, 128)
        )

    loads[0].wait()
    loads[1].wait()

    def hidden(y, carry):
        x = jnp.concatenate(
            [
                g[h, o, y].reshape(CHUNK, CARRY)[:, : WIDTHS[o]]
                for h in range(2)
                for o in range(3)
            ],
            axis=1,
        )
        xe[pl.ds(pl.multiple_of(y * SLOTS, SLOTS), SLOTS)] = jnp.dot(
            place[y], x, preferred_element_type=F32
        ).astype(BF)
        gate = jnp.dot(x, wsg[...], preferred_element_type=F32)
        upper = jnp.dot(x, wsu[...], preferred_element_type=F32)
        share_y = share_s[pl.ds(pl.multiple_of(y * CHUNK, CHUNK), CHUNK)]
        hs = silu(gate) * upper
        lhs[y, :, 0:128] = (hs[:, 0:128] * share_y).astype(BF)
        lhs[y, :, 128:HID] = (hs[:, 128:HID] * share_y[:, 0 : HID - 128]).astype(BF)
        return carry

    lax.fori_loop(0, 4, hidden, 0)

    loads[2].wait()
    loads[3].wait()

    def expert_hidden(i, carry):
        cols = pl.ds(pl.multiple_of(i * 128, 128), 128)
        w = jnp.concatenate([weg[:, cols], weu[:, cols]], axis=1)
        r = jnp.dot(xe[...], w, preferred_element_type=F32)
        he[:, cols] = (silu(r[:, 0:128]) * r[:, 128:256]).astype(BF)
        return carry

    lax.fori_loop(0, HALF // 128, expert_hidden, 0)

    for load in loads[4:]:
        load.wait()

    def expert_down(i, carry):
        h = i // 7
        j = lax.rem(i, 7)
        r = jnp.dot(
            he[...], wed[:, pl.ds(pl.multiple_of(i * 256, 256), 256)], preferred_element_type=F32
        )
        by = pslot[...]
        r = (r * jnp.concatenate([by, by], axis=1)).astype(BF)
        cols = pl.ds(pl.multiple_of(j * 256, 256), 256)
        for y in range(4):
            rhs[h, y, pl.ds(HID, SLOTS), cols] = r[y * SLOTS : (y + 1) * SLOTS]
        return carry

    lax.fori_loop(0, 14, expert_down, 0)

    s, t, u = (s0, s1, s2), (t0, t1, t2), (u0, u1, u2)
    half_in = (a0, a1, a2)
    full_in = (b0, b1, b2)
    last_in = (c0, c1, c2)
    count[0] = 0

    def rsend(src, dst, dev):
        i = count[0]
        count[0] += 1
        c = pltpu.make_async_remote_copy(
            src_ref=src, dst_ref=dst, send_sem=rss.at[i], recv_sem=rsr.at[i],
            device_id=dev, device_id_type=MESH,
        )
        c.start()
        pending.append(c)
        return c

    def combine(o, h, to):
        cols = pl.ds(OFFS[o], WIDTHS[o])

        def step(y, carry):
            r = jnp.dot(lhs[y], rhs[h, y, :, cols], preferred_element_type=F32)
            to[y] = r.astype(BF).reshape(4, 4, PAIR, WIDTHS[o])
            return carry

        lax.fori_loop(0, 4, step, 0)

    sib = []
    for o in range(3):
        combine(o, other, t[o])
        sib.append(rsend(t[o], u[o], sibling))
    for o in range(3):
        combine(o, core, s[o])

    def at1(o, c, half):
        ax = ORDERS[o][2]
        rest = [half, ALL]
        return tuple(c if axis == ax else rest.pop(0) for axis in range(3))

    def add_first(o, c, lo, hi, terms):
        ax = ORDERS[o][2]

        def step(i, carry):
            rest = [i, ALL]
            at = tuple(c if axis == ax else rest.pop(0) for axis in range(3))
            total = s[o][at].astype(F32)
            for term, base in terms:
                total = total + term[i - base].astype(F32)
            s[o][at] = total.astype(BF)
            return carry

        lax.fori_loop(lo, hi, step, 0)

    stage = []
    for o in range(3):
        sib[o].wait_recv()

        def step(i, carry, o=o):
            y = i // 4
            x = lax.rem(i, 4)
            s[o][y, x] = (s[o][y, x].astype(F32) + u[o][y, x].astype(F32)).astype(BF)
            return carry

        lax.fori_loop(0, 16, step, 0)
        ax = ORDERS[o][2]
        so, ha, fu = s[o], half_in[o], full_in[o]
        c1_ = rsend(so.at[at1(o, near(ax, 2), A)], ha.at[0], peer(ax, 1))
        c4_ = rsend(so.at[at1(o, near(ax, 2), B)], ha.at[1], peer(ax, 3))
        c2_ = rsend(so.at[at1(o, near(ax, 1), B)], fu.at[0, B], peer(ax, 1))
        c5_ = rsend(so.at[at1(o, near(ax, 3), A)], fu.at[1, A], peer(ax, 3))
        stage.append([c1_, c4_, c2_, c5_])
    for o in range(3):
        ax = ORDERS[o][2]
        so, ha, fu = s[o], half_in[o], full_in[o]
        stage[o][0].wait_recv()
        add_first(o, near(ax, 1), 0, 2, [(ha.at[0], 0)])
        stage[o].append(rsend(so.at[at1(o, near(ax, 1), A)], fu.at[0, A], peer(ax, 1)))
        stage[o][1].wait_recv()
        add_first(o, near(ax, 3), 2, 4, [(ha.at[1], 2)])
        stage[o].append(rsend(so.at[at1(o, near(ax, 3), B)], fu.at[1, B], peer(ax, 3)))

    def at2(o, c, half):
        return tuple(where_(o, half, c, own[o][2]))

    stage2 = []
    for o in range(3):
        for c in stage[o][2:]:
            c.wait_recv()
        add_first(o, own[o][2], 0, 4, [(full_in[o].at[0], 0), (full_in[o].at[1], 0)])
        ax = ORDERS[o][1]
        so, la = s[o], last_in[o]
        c1_ = rsend(so.at[at2(o, near(ax, 2), A)], la.at[pl.ds(0, 2)], peer(ax, 1))
        c4_ = rsend(so.at[at2(o, near(ax, 2), B)], la.at[pl.ds(2, 2)], peer(ax, 3))
        c2_ = rsend(so.at[at2(o, near(ax, 1), B)], la.at[pl.ds(6, 2)], peer(ax, 1))
        c5_ = rsend(so.at[at2(o, near(ax, 3), A)], la.at[pl.ds(8, 2)], peer(ax, 3))
        stage2.append([c1_, c4_, c2_, c5_])
    for o in range(3):
        ax = ORDERS[o][1]
        so, la = s[o], last_in[o]
        stage2[o][0].wait_recv()
        at = at2(o, near(ax, 1), A)
        so[at] = (so[at].astype(F32) + la[0:2].astype(F32)).astype(BF)
        stage2[o].append(rsend(so.at[at], la.at[pl.ds(4, 2)], peer(ax, 1)))
        stage2[o][1].wait_recv()
        at = at2(o, near(ax, 3), B)
        so[at] = (so[at].astype(F32) + la[2:4].astype(F32)).astype(BF)
        stage2[o].append(rsend(so.at[at], la.at[pl.ds(10, 2)], peer(ax, 3)))

    stage3 = []
    for o in range(3):
        for c in stage2[o][2:]:
            c.wait_recv()
        so, la = s[o], last_in[o]
        at = at2(o, own[o][1], ALL)
        so[at] = (
            so[at].astype(F32) + la[4:8].astype(F32) + la[8:12].astype(F32)
        ).astype(BF)
        ax = ORDERS[o][0]
        stage3.append(
            [
                rsend(
                    so.at[tuple(where_(o, near(ax, k), own[o][1], own[o][2]))],
                    la.at[11 + k],
                    peer(ax, k),
                )
                for k in range(1, 4)
            ]
        )
    for o in range(3):
        total = s[o][pos].astype(F32)
        for k in range(3):
            stage3[o][k].wait_recv()
            total = total + last_in[o][12 + k].astype(F32)
        cols = pl.ds(OFFS[o], WIDTHS[o])
        fin[0, :, cols] = total[0:TOK]
        fin[1, :, cols] = total[TOK:PAIR]

    swap_back = pltpu.make_async_remote_copy(
        src_ref=fin.at[other], dst_ref=rfin, send_sem=x_sem.at[2], recv_sem=x_sem.at[3],
        device_id=sibling, device_id_type=MESH,
    )
    swap_back.start()
    swap_back.wait_recv()
    mine = fin[core]
    theirs = rfin[...]
    ffn_out[:, 0:HALF_D] = jnp.where(first, mine, theirs).astype(BF)
    ffn_out[:, HALF_D:D] = jnp.where(first, theirs, mine).astype(BF)

    for c in zc:
        c.wait_send()
    swap.wait_send()
    swap_back.wait_send()
    for c in pending:
        c.wait_send()


def on_device(
    attn_heads, out_weight, residual, norm_gain, shared_gate, shared_gate_proj, shared_up_proj,
    shared_down_proj, expert_gate, expert_up_weight, expert_down, expert_choice, gate_probs,
):
    vm = pl.BlockSpec(memory_space=pltpu.VMEM)
    hbm = pl.BlockSpec(memory_space=pl.ANY)
    V = pltpu.VMEM
    dma = pltpu.SemaphoreType.DMA
    scratch = [
        V((14, 896, 256), BF), V((D, HID), BF), V((D, HID), BF),
        V((D, HALF), BF), V((D, HALF), BF), V((HALF, D), BF), V((2, 4, 256, HALF_D), BF),
        V((2, 4, TOK, HALF_D), F32), V((4, PAIR, HALF_D), BF), V((3, PAIR, HALF_D), BF),
        V((2, TOK, HALF_D + 128), F32), V((TOK, HALF_D + 128), F32),
        V((2, 3, 4, 4, 4, PAIR, CARRY), BF),
        V((4, SLOTS, CHUNK), BF), V((4 * SLOTS, 128), F32), V((1024, 128), F32),
        V((4, CHUNK, 256), BF), V((4 * SLOTS, D), BF), V((4 * SLOTS, HALF), BF),
    ]
    for _ in range(3):
        scratch += [V((4, 4, 4, PAIR, w), BF) for w in WIDTHS]
    scratch += [V((2, 2, 4, PAIR, w), BF) for w in WIDTHS]
    scratch += [V((2, 4, 4, PAIR, w), BF) for w in WIDTHS]
    scratch += [V((15, PAIR, w), BF) for w in WIDTHS]
    scratch += [V((2, TOK, HALF_D), F32), V((TOK, HALF_D), F32)]
    scratch += [
        dma((14,)), dma((13,)), dma((3,)), dma((3,)), dma((4,)),
        dma((N_AG,)), dma((N_AG,)), dma((N_RS,)), dma((N_RS,)),
    ]
    row = jax.ShapeDtypeStruct((TOK, D), BF)
    return pl.pallas_call(
        kernel,
        out_shape=(row, row),
        in_specs=[vm, hbm, vm, vm, vm, hbm, hbm, hbm, hbm, hbm, hbm, vm, vm],
        out_specs=(vm, vm),
        scratch_shapes=scratch,
        compiler_params=pltpu.CompilerParams(
            collective_id=0, has_side_effects=True, vmem_limit_bytes=63 * 1024 * 1024
        ),
    )(
        attn_heads, out_weight, residual, norm_gain.reshape(1, D), shared_gate.reshape(1, D),
        shared_gate_proj, shared_up_proj, shared_down_proj, expert_gate, expert_up_weight,
        expert_down, expert_choice, gate_probs,
    )


def solution(mesh):
    both = ("dp", "tensor")
    in_specs = (
        P("dp", "tensor"), P("tensor", None), P(both, None), P(), P(),
        P(None, both), P(None, both), P(both, None),
        P(both, None, None), P(both, None, None), P(both, None, None),
        P(both, None), P(both, None),
    )
    out_specs = (P(both, None), P(both, None))
    return jax.shard_map(
        on_device, mesh=mesh, in_specs=in_specs, out_specs=out_specs, check_vma=False
    )
```

time: 820 us -> 107 us (0.13)
  waiting for transfers between devices: 702 us -> 0 us
  Pallas kernels: 0 us -> 95.8 us
  matrix products: 39.1 us -> 0 us
  blocking collectives: 33 us -> 0 us
  between operations: 13.9 us -> 0.65 us
    reduce_scatter x2 -> x0, waiting for transfers between devices: 601 us -> none  [the longest x1 578 us: on_device(): lax.psum_scatter(jnp.dot(block, shared_down_proj, preferred_element_type=...]
    pallas_call x0 -> x1, Pallas kernels: none -> 95.8 us  [on_device(): pl.pallas_call(kernel, out_shape=(row, row), in_specs=[vm, hbm, vm, vm, v...]
    all_gather x1 -> x0, waiting for transfers between devices: 73 us -> none  [on_device(): piece = lax.all_gather(normed, ('dp', 'tensor'), axis=0, tiled=True)]
    dot_general x10 -> x0, matrix products: 39.1 us -> none  [the longest x1 12.8 us: on_device(): jnp.dot(block, shared_down_proj, preferred_element_type=jnp.float32)]
    all_to_all x1 -> x0, blocking collectives: 33 us -> none  [on_device(): lax.all_to_all(outgoing, ('dp', 'tensor'), split_axis=0, concat_axis=0, t...]
    all_to_all x1 -> x0, waiting for transfers between devices: 27.4 us -> none  [on_device(): lax.all_to_all(expert_out, ('dp', 'tensor'), split_axis=0, concat_axis=0,...]
    reshape x3 -> x2, local copies, waits for them, and re-layouts: 12.7 us -> 2.7 us  [the longest x1 1.4 us: on_device(): norm_gain.reshape(1, D)]
  transfers between devices with their start and end apart: 4 -> 0, of which waited for: 4 -> 0; matrix products, arithmetic and copies ran while one was open for 4% -> 0% of each run, Pallas kernels for 0% -> 0%
where the time goes in v1:
time: 107 us; the launch traced here: 106 us
  Pallas kernels  95.8 us (90%)
  local copies, waits for them, and re-layouts  9.89 us (9%)
    pallas_call x1, Pallas kernels, on_device(): pl.pallas_call(kernel, out_shape=(row, row), in_specs=[vm, hbm, vm, vm, v...  95.8 us
    unnamed x6, local copies, waits for them, and re-layouts  7.19 us

profile of v1, /device:TPU:1, one launch (start us, length us, event | category | flops | bytes accessed | tf_op | source)
XLA Modules:
  0.0 106.3 jit_solution(16039731137800919727)
XLA Ops:
  0.6 0.0 copy-start
  0.6 1.4 %reshape.10.gain = bf16[1,3584]{1,0:T(2,128)(2,1)} reshape(bf16[3584]{0:T(1024)(128)(2,1)} %param.16) | data formatting | bytes 14336 | tf_op jit(solution)/shard_map/reshape | solution.py:531
  2.0 1.3 %reshape.11.sgate = bf16[1,3584]{1,0:T(2,128)(2,1)} reshape(bf16[3584]{0:T(1024)(128)(2,1)} %param.17) | data formatting | bytes 14336 | tf_op jit(solution)/shard_map/reshape | solution.py:531
  3.3 2.6 %copy.15.sgp = bf16[3584,160]{1,0:T(8,128)(2,1)} copy(bf16[3584,160]{0,1:T(8,128)(2,1)} %param.18) | data formatting | bytes 2293760 | tf_op args[5]
  6.0 0.0 copy-done
  6.0 1.7 %copy.16.sup = bf16[3584,160]{1,0:T(8,128)(2,1)} copy(bf16[3584,160]{0,1:T(8,128)(2,1)S(1)} %copy-done) | data formatting | bytes 2293760 | tf_op args[6]
  7.6 95.8 %shard_map.140 = (bf16[8,3584]{1,0:T(8,128)(2,1)}, bf16[8,3584]{1,0:T(8,128)(2,1)}) custom-call(bf16[32,896]{1,0:T(8,128)(2,1)} %heads.1, bf16[896,3584]{1,0:T(8,128)(2,1)} %out_w.1, bf16[8,3584]{1,0:T(8,128)(2,1)} %residual.1, bf16[1,3584]{1,0:T(2,128)(2,1)} %reshape.10.gain, bf16[1,3584]{1,0:T(2,128)(2,1)} %reshape.11.sgate, bf16[3584,160]{1,0:T(8,128)(2,1)} %copy.15.sgp, ...), custom_call_target="tpu_custom_call" | custom-call | tf_op jit(solution)/shard_map/pallas_call | solution.py:521
  103.4 1.4 %copy.19 = bf16[8,3584]{1,0:T(8,128)(2,1)} copy(bf16[8,3584]{1,0:T(8,128)(2,1)} %get-tuple-element.4) | data formatting | bytes 114688
  104.9 1.4 %copy.20 = bf16[8,3584]{1,0:T(8,128)(2,1)} copy(bf16[8,3584]{1,0:T(8,128)(2,1)} %get-tuple-element.5) | data formatting | bytes 114688
Async XLA Ops:
  0.6 5.4 %copy-start = (bf16[3584,160]{0,1:T(8,128)(2,1)S(1)}, bf16[3584,160]{0,1:T(8,128)(2,1)}, u32[]{:S(2)}) copy-start(bf16[3584,160]{0,1:T(8,128)(2,1)} %param.19) | copy-start | bytes 3440644

commit v2 on v1

v2 whole, which is shorter than its diff:
```python
import jax
import jax.numpy as jnp
from jax import lax
from jax.experimental import pallas as pl
from jax.experimental.pallas import tpu as pltpu
from jax.sharding import PartitionSpec as P

MESH = pl.DeviceIdType.MESH
BF = jnp.bfloat16
F32 = jnp.float32
TOK = 8
PAIR = 16
D = 3584
HALF_D = D // 2
WIDTHS = (640, 640, 512)
OFFS = (0, 640, 1280)
CARRY = 640
ORDERS = ((2, 1, 0), (1, 0, 2), (0, 2, 1))
HID = 160
HALF = 640
EXPERTS = 64
CHUNK = 256
SLOTS = 64
N_AG = 3 * (3 + 3 + 6 + 7)
N_RS = 3 * (4 + 6 + 3 + 3)


def silu(v):
    return v / (1.0 + jnp.exp(-v))


def kernel(
    heads, out_w, residual, gain, sgate, sgp, sup, sdn, eg, eu, ed, choice, probs,
    both_out,
    wo, wsg, wsu, weg, weu, wed, rhs,
    part, sbuf, rz, nx, rx, g,
    acc_g, acc_u, place, pslot, share_s, lhs, xe, he,
    s0, s1, s2, t0, t1, t2, u0, u1, u2,
    a0, a1, a2, b0, b1, b2, c0, c1, c2, d0, d1, d2,
    fin, rfin,
    w_sem, again_sem, zs_sem, zr_sem, x_sem, ags, agr, rss, rsr,
):
    dp = lax.axis_index("dp")
    z0 = lax.axis_index("tensor")
    core = lax.rem(dp, 2)
    other = 1 - core
    pos = (dp // 8, lax.rem(dp // 2, 4), z0)

    def device(y, x, c, z):
        return ((y * 4 + x) * 2 + c, z)

    def near(axis, k):
        return lax.rem(pos[axis] + k, 4)

    def peer(axis, k):
        at = list(pos)
        at[axis] = near(axis, k)
        return device(at[0], at[1], core, at[2])

    sibling = device(pos[0], pos[1], other, pos[2])

    wo_load = pltpu.make_async_copy(out_w, wo, w_sem.at[0])
    loads = [
        pltpu.make_async_copy(sgp, wsg, w_sem.at[1]),
        pltpu.make_async_copy(sup, wsu, w_sem.at[2]),
        pltpu.make_async_copy(eg.at[0], weg, w_sem.at[3]),
        pltpu.make_async_copy(eu.at[0], weu, w_sem.at[4]),
        pltpu.make_async_copy(ed.at[0], wed, w_sem.at[5]),
    ]
    for h in range(2):
        cols = pl.ds(h * HALF_D, HALF_D)
        loads.append(
            pltpu.make_async_copy(sdn.at[:, cols], rhs.at[h, 0, pl.ds(0, HID)], w_sem.at[6 + h])
        )
    wo_load.start()
    for load in loads[0:4]:
        load.start()

    barrier = pltpu.get_barrier_semaphore()
    for axis in range(3):
        for k in range(1, 4):
            pl.semaphore_signal(barrier, inc=1, device_id=peer(axis, k), device_id_type=MESH)
    pl.semaphore_signal(barrier, inc=1, device_id=sibling, device_id_type=MESH)

    def project(j, carry):
        at = pl.multiple_of(j * 256, 256)
        cols = pl.ds(at, 256)
        left = jnp.dot(heads[...], wo[:, cols], preferred_element_type=F32)
        right = jnp.dot(
            heads[...], wo[:, pl.ds(at + HALF_D, 256)], preferred_element_type=F32
        )
        part[0, :, :, cols] = left.reshape(4, TOK, 256)
        part[1, :, :, cols] = right.reshape(4, TOK, 256)
        for q in range(4):
            rows = slice(q * TOK, (q + 1) * TOK)
            sbuf[q, :, cols] = jnp.concatenate([left[rows], right[rows]], axis=0).astype(BF)
        return carry

    wo_load.wait()
    lax.fori_loop(0, 7, project, 0)

    pl.semaphore_wait(barrier, 10)

    zc = []
    for k in range(1, 4):
        c = pltpu.make_async_remote_copy(
            src_ref=sbuf.at[near(2, k)], dst_ref=rz.at[k - 1],
            send_sem=zs_sem.at[k - 1], recv_sem=zr_sem.at[k - 1],
            device_id=peer(2, k), device_id_type=MESH,
        )
        c.start()
        zc.append(c)

    rhs[:, :, HID:256, :] = jnp.zeros((2, 4, 256 - HID, HALF_D), BF)

    for c in zc:
        c.wait_recv()

    square = jnp.zeros((TOK, 1), F32)
    mids = []
    for h in range(2):
        cols = slice(h * HALF_D, (h + 1) * HALF_D)
        total = part[h, z0]
        for k in range(3):
            total = total + rz[k].astype(F32)[h * TOK : (h + 1) * TOK]
        mid = (residual[:, cols].astype(F32) + total).astype(BF)
        both_out[0, :, cols] = mid
        midf = mid.astype(F32)
        mids.append(midf)
        square = square + jnp.sum(midf * midf, axis=1, keepdims=True)
    scale = lax.rsqrt(square * (1.0 / D) + 1e-06)
    logit = jnp.zeros((TOK, 1), F32)
    for h in range(2):
        cols = slice(h * HALF_D, (h + 1) * HALF_D)
        normed = (mids[h] * scale * gain[cols].astype(F32).reshape(1, HALF_D)).astype(BF).astype(F32)
        nx[h, :, 0:HALF_D] = normed
        logit = logit + jnp.sum(normed * sgate[cols].astype(F32).reshape(1, HALF_D), axis=1, keepdims=True)
    share = 1.0 / (1.0 + jnp.exp(-logit))

    lane = lax.broadcasted_iota(jnp.int32, (TOK, 128), 1)
    facts = jnp.zeros((TOK, 128), F32)
    chosen = choice[...].astype(F32)
    weight = probs[...]
    high = weight.astype(BF).astype(F32)
    low = weight - high
    for k in range(8):
        facts = jnp.where(lane == k, chosen[:, k : k + 1], facts)
        facts = jnp.where(lane == 8 + k, high[:, k : k + 1], facts)
        facts = jnp.where(lane == 16 + k, low[:, k : k + 1], facts)
    share_high = share.astype(BF).astype(F32)
    facts = jnp.where(lane == 24, share_high, facts)
    facts = jnp.where(lane == 25, share - share_high, facts)
    for h in range(2):
        nx[h, :, HALF_D : HALF_D + 128] = facts

    swap = pltpu.make_async_remote_copy(
        src_ref=nx.at[other], dst_ref=rx, send_sem=x_sem.at[0], recv_sem=x_sem.at[1],
        device_id=sibling, device_id_type=MESH,
    )
    swap.start()
    swap.wait_recv()
    mine = nx[core]
    theirs = rx[...]
    first = core == 0
    block = jnp.concatenate(
        [jnp.where(first, mine, theirs), jnp.where(first, theirs, mine)], axis=0
    ).astype(BF)
    for o in range(3):
        g[core, o, pos[0], pos[1], pos[2]] = block[:, o * CARRY : (o + 1) * CARRY]

    again = []
    for h in range(2):
        for y in range(1, 4):
            again.append(
                pltpu.make_async_copy(
                    rhs.at[h, 0, pl.ds(0, HID)], rhs.at[h, y, pl.ds(0, HID)],
                    again_sem.at[h * 3 + y - 1],
                )
            )

    pending = []
    count = [0]

    def gsend(o, at, dev):
        i = count[0]
        count[0] += 1
        ref = g.at[(core, o) + tuple(at)]
        c = pltpu.make_async_remote_copy(
            src_ref=ref, dst_ref=ref, send_sem=ags.at[i], recv_sem=agr.at[i],
            device_id=dev, device_id_type=MESH,
        )
        c.start()
        pending.append(c)
        return c

    def where_(o, first_, second, third):
        at = [None, None, None]
        for axis, v in zip(ORDERS[o], (first_, second, third)):
            at[axis] = v
        return at

    ALL, A, B = pl.ds(0, 4), pl.ds(0, 2), pl.ds(2, 2)
    own = [[pos[axis] for axis in ORDERS[o]] for o in range(3)]

    got = [[gsend(o, pos, peer(ORDERS[o][0], k)) for k in (1, 3, 2)] for o in range(3)]
    for load in loads[4:]:
        load.start()
    acc_g[...] = jnp.zeros((4, 4, 4, PAIR, HID), F32)
    acc_u[...] = jnp.zeros((4, 4, 4, PAIR, HID), F32)
    for load in loads[0:4]:
        load.wait()

    def absorb(h, o, k):
        at = tuple(where_(o, ALL, ALL, near(ORDERS[o][2], k)))
        x = g[(h, o) + at].reshape(CHUNK, CARRY)[:, : WIDTHS[o]]
        cols = pl.ds(pl.multiple_of(h * HALF_D + OFFS[o], 128), WIDTHS[o])
        turn = (((1,), (1,)), ((), ()))
        for acc, w in ((acc_g, wsg), (acc_u, wsu)):
            r = lax.dot_general(x, w[:, cols], turn, preferred_element_type=F32)
            acc[at] = acc[at] + r.reshape(4, 4, PAIR, HID)

    hop = []
    for o in range(3):
        for c in got[o]:
            c.wait_recv()
        mine_at = where_(o, ALL, own[o][1], own[o][2])
        hop.append([gsend(o, mine_at, peer(ORDERS[o][1], k)) for k in (1, 3, 2)])
    for load in loads[4:]:
        load.wait()
    for copy in again:
        copy.start()
    stage = []
    sib = [[], [], []]
    for o in range(3):
        for c in hop[o]:
            c.wait_recv()
        ax = ORDERS[o][2]
        at_a = where_(o, A, ALL, own[o][2])
        at_b = where_(o, B, ALL, own[o][2])
        ra = gsend(o, at_a, peer(ax, 1))
        lb = gsend(o, at_b, peer(ax, 3))
        rb = gsend(o, at_b, peer(ax, 1))
        la = gsend(o, at_a, peer(ax, 3))
        stage.append((ra, lb, rb, la))
        sib[o].append(gsend(o, where_(o, ALL, ALL, own[o][2]), sibling))
    for o in range(3):
        absorb(core, o, 0)
    for o in range(3):
        sib[o][0].wait_recv()
        absorb(other, o, 0)
    hop = [[], [], []]
    for event in range(4):
        for o in range(3):
            ax = ORDERS[o][2]
            half = (A, B, B, A)[event]
            came = near(ax, (3, 1, 3, 1)[event])
            at = where_(o, half, ALL, came)
            stage[o][event].wait_recv()
            if event < 2:
                hop[o].append(gsend(o, at, peer(ax, (1, 3)[event])))
            sib[o].append(gsend(o, at, sibling))
    for o in range(3):
        absorb(core, o, 3)
        absorb(core, o, 1)
    for o in range(3):
        sib[o][1].wait_recv()
        sib[o][3].wait_recv()
        absorb(other, o, 3)
        sib[o][2].wait_recv()
        sib[o][4].wait_recv()
        absorb(other, o, 1)
    for event in range(2):
        for o in range(3):
            ax = ORDERS[o][2]
            hop[o][event].wait_recv()
            sib[o].append(gsend(o, where_(o, (A, B)[event], ALL, near(ax, 2)), sibling))
    for o in range(3):
        absorb(core, o, 2)
    for o in range(3):
        sib[o][5].wait_recv()
        sib[o][6].wait_recv()
        absorb(other, o, 2)

    expert = lax.rem(dp * 4 + z0, EXPERTS).astype(F32)
    told = g[0, 2, :, :, :, :, 512:640].reshape(1024, 128).astype(F32)
    share_s[...] = jnp.broadcast_to(told[:, 24:25] + told[:, 25:26], (1024, 128))
    turned = told.T
    hit8 = turned[0:8] == expert
    p_row = jnp.sum(jnp.where(hit8, turned[8:16] + turned[16:24], 0.0), axis=0, keepdims=True)
    hit = jnp.sum(jnp.where(hit8, 1.0, 0.0), axis=0, keepdims=True)
    hit = jnp.broadcast_to(hit, (8, 1024))
    token = lax.broadcasted_iota(jnp.int32, (8, 1024), 1)
    rank = jnp.zeros((8, 1024), F32)
    for k in range(1, 8):
        rank = rank + jnp.where(lax.rem(token, 8) >= k, pltpu.roll(hit, k, axis=1), 0.0)
    row = (lax.rem(token // 8, 32) * 2).astype(F32) + rank
    row = jnp.where(hit > 0.5, row, -1000.0)
    row1 = row[0:1]
    column = jnp.broadcast_to(row1, (128, 1024)).T
    lane1 = lax.broadcasted_iota(jnp.int32, (1024, 128), 1).astype(F32)
    lhs[:, :, 0:128] = jnp.zeros((4, CHUNK, 128), BF)
    lhs[:, :, 128:256] = (
        jnp.where(lane1 - (HID - 128.0) == column, 1.0, 0.0).astype(BF).reshape(4, CHUNK, 128)
    )
    slot_id = lax.broadcasted_iota(jnp.int32, (SLOTS, CHUNK), 0).astype(F32)
    for y in range(4):
        cols = slice(y * CHUNK, (y + 1) * CHUNK)
        chosen_y = jnp.where(slot_id == row1[:, cols], 1.0, 0.0)
        place[y] = chosen_y.astype(BF)
        pslot[pl.ds(y * SLOTS, SLOTS)] = jnp.broadcast_to(
            jnp.sum(chosen_y * p_row[:, cols], axis=1, keepdims=True), (SLOTS, 128)
        )

    def hidden(y, carry):
        x = jnp.concatenate(
            [
                g[h, o, y].reshape(CHUNK, CARRY)[:, : WIDTHS[o]]
                for h in range(2)
                for o in range(3)
            ],
            axis=1,
        )
        xe[pl.ds(pl.multiple_of(y * SLOTS, SLOTS), SLOTS)] = jnp.dot(
            place[y], x, preferred_element_type=F32
        ).astype(BF)
        share_y = share_s[pl.ds(pl.multiple_of(y * CHUNK, CHUNK), CHUNK)]
        hs = silu(acc_g[y].reshape(CHUNK, HID)) * acc_u[y].reshape(CHUNK, HID)
        lhs[y, :, 0:128] = (hs[:, 0:128] * share_y).astype(BF)
        lhs[y, :, 128:HID] = (hs[:, 128:HID] * share_y[:, 0 : HID - 128]).astype(BF)
        return carry

    lax.fori_loop(0, 4, hidden, 0, unroll=True)

    def expert_hidden(i, carry):
        cols = pl.ds(pl.multiple_of(i * 128, 128), 128)
        w = jnp.concatenate([weg[:, cols], weu[:, cols]], axis=1)
        r = jnp.dot(xe[...], w, preferred_element_type=F32)
        he[:, cols] = (silu(r[:, 0:128]) * r[:, 128:256]).astype(BF)
        return carry

    lax.fori_loop(0, HALF // 128, expert_hidden, 0, unroll=True)

    for copy in again:
        copy.wait()

    by = jnp.concatenate([pslot[...]] * 4, axis=1)
    for h in range(2):
        for at, w in ((0, 512), (512, 512), (1024, 512), (1536, 256)):
            r = jnp.dot(
                he[...], wed[:, h * HALF_D + at : h * HALF_D + at + w], preferred_element_type=F32
            )
            r = (r * by[:, 0:w]).astype(BF)
            for y in range(4):
                rhs[h, y, HID : HID + SLOTS, at : at + w] = r[y * SLOTS : (y + 1) * SLOTS]

    s, t, u = (s0, s1, s2), (t0, t1, t2), (u0, u1, u2)
    half_in = (a0, a1, a2)
    full_in = (b0, b1, b2)
    last_in = (c0, c1, c2)
    one_in = (d0, d1, d2)
    count[0] = 0

    def rsend(src, dst, dev):
        i = count[0]
        count[0] += 1
        c = pltpu.make_async_remote_copy(
            src_ref=src, dst_ref=dst, send_sem=rss.at[i], recv_sem=rsr.at[i],
            device_id=dev, device_id_type=MESH,
        )
        c.start()
        pending.append(c)
        return c

    def combine(o, h, to):
        cols = slice(OFFS[o], OFFS[o] + WIDTHS[o])
        for y in range(4):
            r = jnp.dot(lhs[y], rhs[h, y, :, cols], preferred_element_type=F32)
            to[y] = r.astype(BF).reshape(4, 4, PAIR, WIDTHS[o])

    def at1(o, c, half):
        rest = [half, ALL]
        return tuple(c if axis == ORDERS[o][2] else rest.pop(0) for axis in range(3))

    def add1(o, c, lo, hi, terms):
        def step(i, carry):
            at = at1(o, c, i)
            total = s[o][at].astype(F32) + u[o][at].astype(F32)
            for term, base in terms:
                total = total + term[i - base].astype(F32)
            s[o][at] = total.astype(BF)
            return carry

        lax.fori_loop(lo, hi, step, 0)

    for o in range(3):
        combine(o, other, t[o])
    sib = [[], [], []]
    for k in (2, 1, 3, 0):
        for o in range(3):
            at = at1(o, near(ORDERS[o][2], k), ALL)
            sib[o].append(rsend(t[o].at[at], u[o].at[at], sibling))
    for o in range(3):
        combine(o, core, s[o])

    stage = [[], [], []]
    for o in range(3):
        ax = ORDERS[o][2]
        c = near(ax, 2)
        sib[o][0].wait_recv()
        add1(o, c, 0, 2, [])
        stage[o].append(rsend(s[o].at[at1(o, c, A)], half_in[o].at[0], peer(ax, 1)))
        add1(o, c, 2, 4, [])
        stage[o].append(rsend(s[o].at[at1(o, c, B)], half_in[o].at[1], peer(ax, 3)))
    for o in range(3):
        ax = ORDERS[o][2]
        c = near(ax, 1)
        sib[o][1].wait_recv()
        add1(o, c, 2, 4, [])
        stage[o].append(rsend(s[o].at[at1(o, c, B)], full_in[o].at[0, B], peer(ax, 1)))
        c = near(ax, 3)
        sib[o][2].wait_recv()
        add1(o, c, 0, 2, [])
        stage[o].append(rsend(s[o].at[at1(o, c, A)], full_in[o].at[1, A], peer(ax, 3)))
    for o in range(3):
        ax = ORDERS[o][2]
        c = near(ax, 1)
        stage[o][0].wait_recv()
        add1(o, c, 0, 2, [(half_in[o].at[0], 0)])
        stage[o].append(rsend(s[o].at[at1(o, c, A)], full_in[o].at[0, A], peer(ax, 1)))
        c = near(ax, 3)
        stage[o][1].wait_recv()
        add1(o, c, 2, 4, [(half_in[o].at[1], 2)])
        stage[o].append(rsend(s[o].at[at1(o, c, B)], full_in[o].at[1, B], peer(ax, 3)))

    def at2(o, c):
        return tuple(where_(o, ALL, c, own[o][2]))

    stage2 = []
    for o in range(3):
        sib[o][3].wait_recv()
        for c in stage[o][2:]:
            c.wait_recv()
        add1(o, own[o][2], 0, 4, [(full_in[o].at[0], 0), (full_in[o].at[1], 0)])
        ax = ORDERS[o][1]
        stage2.append(
            [
                rsend(s[o].at[at2(o, near(ax, k))], last_in[o].at[k - 1], peer(ax, k))
                for k in (1, 3, 2)
            ]
        )

    stage3 = []
    for o in range(3):
        for c in stage2[o]:
            c.wait_recv()
        at = at2(o, own[o][1])
        total = s[o][at].astype(F32)
        for k in range(3):
            total = total + last_in[o][k].astype(F32)
        s[o][at] = total.astype(BF)
        ax = ORDERS[o][0]
        stage3.append(
            [
                rsend(
                    s[o].at[tuple(where_(o, near(ax, k), own[o][1], own[o][2]))],
                    one_in[o].at[k - 1],
                    peer(ax, k),
                )
                for k in (1, 2, 3)
            ]
        )
    for o in range(3):
        total = s[o][pos].astype(F32)
        for k in range(3):
            stage3[o][k].wait_recv()
            total = total + one_in[o][k].astype(F32)
        cols = pl.ds(OFFS[o], WIDTHS[o])
        fin[0, :, cols] = total[0:TOK]
        fin[1, :, cols] = total[TOK:PAIR]

    swap_back = pltpu.make_async_remote_copy(
        src_ref=fin.at[other], dst_ref=rfin, send_sem=x_sem.at[2], recv_sem=x_sem.at[3],
        device_id=sibling, device_id_type=MESH,
    )
    swap_back.start()
    swap_back.wait_recv()
    mine = fin[core]
    theirs = rfin[...]
    both_out[1, :, 0:HALF_D] = jnp.where(first, mine, theirs).astype(BF)
    both_out[1, :, HALF_D:D] = jnp.where(first, theirs, mine).astype(BF)

    for c in zc:
        c.wait_send()
    swap.wait_send()
    swap_back.wait_send()
    for c in pending:
        c.wait_send()


def on_device(
    attn_heads, out_weight, residual, norm_gain, shared_gate, shared_gate_proj, shared_up_proj,
    shared_down_proj, expert_gate, expert_up_weight, expert_down, expert_choice, gate_probs,
):
    vm = pl.BlockSpec(memory_space=pltpu.VMEM)
    hbm = pl.BlockSpec(memory_space=pl.ANY)
    V = pltpu.VMEM
    dma = pltpu.SemaphoreType.DMA
    scratch = [
        V((896, D), BF), V((HID, D), BF), V((HID, D), BF),
        V((D, HALF), BF), V((D, HALF), BF), V((HALF, D), BF), V((2, 4, 256, HALF_D), BF),
        V((2, 4, TOK, HALF_D), F32), V((4, PAIR, HALF_D), BF), V((3, PAIR, HALF_D), BF),
        V((2, TOK, HALF_D + 128), F32), V((TOK, HALF_D + 128), F32),
        V((2, 3, 4, 4, 4, PAIR, CARRY), BF),
        V((4, 4, 4, PAIR, HID), F32), V((4, 4, 4, PAIR, HID), F32),
        V((4, SLOTS, CHUNK), BF), V((4 * SLOTS, 128), F32), V((1024, 128), F32),
        V((4, CHUNK, 256), BF), V((4 * SLOTS, D), BF), V((4 * SLOTS, HALF), BF),
    ]
    for _ in range(3):
        scratch += [V((4, 4, 4, PAIR, w), BF) for w in WIDTHS]
    scratch += [V((2, 2, 4, PAIR, w), BF) for w in WIDTHS]
    scratch += [V((2, 4, 4, PAIR, w), BF) for w in WIDTHS]
    scratch += [V((3, 4, PAIR, w), BF) for w in WIDTHS]
    scratch += [V((3, PAIR, w), BF) for w in WIDTHS]
    scratch += [V((2, TOK, HALF_D), F32), V((TOK, HALF_D), F32)]
    scratch += [
        dma((8,)), dma((6,)), dma((3,)), dma((3,)), dma((4,)),
        dma((N_AG,)), dma((N_AG,)), dma((N_RS,)), dma((N_RS,)),
    ]
    both = pl.pallas_call(
        kernel,
        out_shape=jax.ShapeDtypeStruct((2, TOK, D), BF),
        in_specs=[vm, hbm, vm, vm, vm, hbm, hbm, hbm, hbm, hbm, hbm, vm, vm],
        out_specs=vm,
        scratch_shapes=scratch,
        compiler_params=pltpu.CompilerParams(
            collective_id=0, has_side_effects=True, vmem_limit_bytes=63 * 1024 * 1024
        ),
    )(
        attn_heads, out_weight, residual, norm_gain, shared_gate,
        shared_gate_proj.T, shared_up_proj.T, shared_down_proj, expert_gate, expert_up_weight,
        expert_down, expert_choice, gate_probs,
    )
    return both[0], both[1]


def solution(mesh):
    both = ("dp", "tensor")
    in_specs = (
        P("dp", "tensor"), P("tensor", None), P(both, None), P(), P(),
        P(None, both), P(None, both), P(both, None),
        P(both, None, None), P(both, None, None), P(both, None, None),
        P(both, None), P(both, None),
    )
    out_specs = (P(both, None), P(both, None))
    return jax.shard_map(
        on_device, mesh=mesh, in_specs=in_specs, out_specs=out_specs, check_vma=False
    )
```

time: 107 us -> 82.4 us (0.77)
  Pallas kernels: 95.8 us -> 80 us
  local copies, waits for them, and re-layouts: 9.89 us -> 1.49 us
    pallas_call x1, Pallas kernels: 95.8 us -> 80 us  [on_device(): pl.pallas_call(kernel, out_shape=jax.ShapeDtypeStruct((2, TOK, D), BF), i...]
    unnamed x6 -> x0, local copies, waits for them, and re-layouts: 7.19 us -> none
    reshape x2 -> x0, local copies, waits for them, and re-layouts: 2.7 us -> none  [the longest x1 1.4 us: on_device(): norm_gain.reshape(1, D)]
    squeeze x0 -> x1, local copies, waits for them, and re-layouts: none -> 1.49 us  [on_device(): return (both[0], both[1])]
where the time goes in v2:
time: 82.4 us; the launch traced here: 82.2 us
  Pallas kernels  80 us (97%)
  local copies, waits for them, and re-layouts  1.49 us (2%)
    pallas_call x1, Pallas kernels, on_device(): pl.pallas_call(kernel, out_shape=jax.ShapeDtypeStruct((2, TOK, D), BF), i...  80 us

profile of v2, /device:TPU:1, one launch (start us, length us, event | category | flops | bytes accessed | tf_op | source)
XLA Modules:
  0.0 82.2 jit_solution(8970751219295002800)
XLA Ops:
  0.6 80.0 %shard_map.140 = bf16[2,8,3584]{2,1,0:T(8,128)(2,1)} custom-call(bf16[32,896]{1,0:T(8,128)(2,1)} %heads.1, bf16[896,3584]{1,0:T(8,128)(2,1)} %out_w.1, bf16[8,3584]{1,0:T(8,128)(2,1)} %residual.1, bf16[3584]{0:T(1024)(128)(2,1)} %gain.1, bf16[3584]{0:T(1024)(128)(2,1)} %sgate.1, bf16[160,3584]{1,0:T(8,128)(2,1)} %bitcast.6, bf16[160,3584]{1,0:T(8,128)(2,1)} %bitcast.7, ...), custom_call_target="tpu_custom_call" | custom-call | tf_op jit(solution)/shard_map/pallas_call | solution.py:529
  80.7 1.5 %slice_bitcast_fusion = (bf16[8,3584]{1,0:T(8,128)(2,1)}, bf16[8,3584]{1,0:T(8,128)(2,1)}) fusion(bf16[2,8,3584]{2,1,0:T(8,128)(2,1)} %shard_map.140), kind=kLoop, calls=%fused_computation | loop fusion | bytes 229376 | tf_op jit(solution)/shard_map/squeeze | solution.py:543

commit v3 on v2

--- a/solution.py
+++ b/solution.py
@@ -21,8 +21,8 @@
 EXPERTS = 64
 CHUNK = 256
 SLOTS = 64
-N_AG = 3 * (3 + 3 + 6 + 7)
-N_RS = 3 * (4 + 6 + 3 + 3)
+N_AG = 3 * (3 + 3 + 6 + 4)
+N_RS = 3 * (6 + 3 + 3)
 
 
 def silu(v):
@@ -34,11 +34,11 @@
     both_out,
     wo, wsg, wsu, weg, weu, wed, rhs,
     part, sbuf, rz, nx, rx, g,
-    acc_g, acc_u, place, pslot, share_s, lhs, xe, he,
-    s0, s1, s2, t0, t1, t2, u0, u1, u2,
+    wd, res, lhs_in, acc_g, acc_u, place, pslot, share_s, lhs, xe, he,
+    s0, s1, s2,
     a0, a1, a2, b0, b1, b2, c0, c1, c2, d0, d1, d2,
     fin, rfin,
-    w_sem, again_sem, zs_sem, zr_sem, x_sem, ags, agr, rss, rsr,
+    w_sem, again_sem, sib_s, sib_r, zs_sem, zr_sem, x_sem, ags, agr, rss, rsr,
 ):
     dp = lax.axis_index("dp")
     z0 = lax.axis_index("tensor")
@@ -69,9 +69,7 @@
     ]
     for h in range(2):
         cols = pl.ds(h * HALF_D, HALF_D)
-        loads.append(
-            pltpu.make_async_copy(sdn.at[:, cols], rhs.at[h, 0, pl.ds(0, HID)], w_sem.at[6 + h])
-        )
+        loads.append(pltpu.make_async_copy(sdn.at[:, cols], wd.at[h], w_sem.at[6 + h]))
     wo_load.start()
     for load in loads[0:4]:
         load.start()
@@ -97,7 +95,7 @@
         return carry
 
     wo_load.wait()
-    lax.fori_loop(0, 7, project, 0)
+    lax.fori_loop(0, 7, project, 0, unroll=True)
 
     pl.semaphore_wait(barrier, 10)
 
@@ -111,7 +109,18 @@
         c.start()
         zc.append(c)
 
-    rhs[:, :, HID:256, :] = jnp.zeros((2, 4, 256 - HID, HALF_D), BF)
+    rhs[:, :, HID + SLOTS : 256, :] = jnp.zeros((2, 4, 256 - HID - SLOTS, HALF_D), BF)
+
+    lane = lax.broadcasted_iota(jnp.int32, (TOK, 128), 1)
+    facts = jnp.zeros((TOK, 128), F32)
+    chosen = choice[...].astype(F32)
+    weight = probs[...]
+    high = weight.astype(BF).astype(F32)
+    low = weight - high
+    for k in range(8):
+        facts = jnp.where(lane == k, chosen[:, k : k + 1], facts)
+        facts = jnp.where(lane == 8 + k, high[:, k : k + 1], facts)
+        facts = jnp.where(lane == 16 + k, low[:, k : k + 1], facts)
 
     for c in zc:
         c.wait_recv()
@@ -137,16 +146,6 @@
         logit = logit + jnp.sum(normed * sgate[cols].astype(F32).reshape(1, HALF_D), axis=1, keepdims=True)
     share = 1.0 / (1.0 + jnp.exp(-logit))
 
-    lane = lax.broadcasted_iota(jnp.int32, (TOK, 128), 1)
-    facts = jnp.zeros((TOK, 128), F32)
-    chosen = choice[...].astype(F32)
-    weight = probs[...]
-    high = weight.astype(BF).astype(F32)
-    low = weight - high
-    for k in range(8):
-        facts = jnp.where(lane == k, chosen[:, k : k + 1], facts)
-        facts = jnp.where(lane == 8 + k, high[:, k : k + 1], facts)
-        facts = jnp.where(lane == 16 + k, low[:, k : k + 1], facts)
     share_high = share.astype(BF).astype(F32)
     facts = jnp.where(lane == 24, share_high, facts)
     facts = jnp.where(lane == 25, share - share_high, facts)
@@ -169,14 +168,18 @@
         g[core, o, pos[0], pos[1], pos[2]] = block[:, o * CARRY : (o + 1) * CARRY]
 
     again = []
-    for h in range(2):
-        for y in range(1, 4):
-            again.append(
-                pltpu.make_async_copy(
-                    rhs.at[h, 0, pl.ds(0, HID)], rhs.at[h, y, pl.ds(0, HID)],
-                    again_sem.at[h * 3 + y - 1],
-                )
-            )
+    for y in range(4):
+        again.append(
+            pltpu.make_async_copy(wd.at[core], rhs.at[0, y, pl.ds(0, HID)], again_sem.at[y])
+        )
+
+    def to_sibling(i, src, dst):
+        return pltpu.make_async_remote_copy(
+            src_ref=src, dst_ref=dst, send_sem=sib_s.at[i], recv_sem=sib_r.at[i],
+            device_id=sibling, device_id_type=MESH,
+        )
+
+    across = [to_sibling(y, wd.at[other], rhs.at[1, y, pl.ds(0, HID)]) for y in range(4)]
 
     pending = []
     count = [0]
@@ -227,7 +230,7 @@
         hop.append([gsend(o, mine_at, peer(ORDERS[o][1], k)) for k in (1, 3, 2)])
     for load in loads[4:]:
         load.wait()
-    for copy in again:
+    for copy in again + across:
         copy.start()
     stage = []
     sib = [[], [], []]
@@ -258,31 +261,23 @@
             stage[o][event].wait_recv()
             if event < 2:
                 hop[o].append(gsend(o, at, peer(ax, (1, 3)[event])))
-            sib[o].append(gsend(o, at, sibling))
+            if event >= 2:
+                sib[o].append(gsend(o, where_(o, ALL, ALL, came), sibling))
     for o in range(3):
         absorb(core, o, 3)
         absorb(core, o, 1)
     for o in range(3):
         sib[o][1].wait_recv()
-        sib[o][3].wait_recv()
         absorb(other, o, 3)
         sib[o][2].wait_recv()
-        sib[o][4].wait_recv()
         absorb(other, o, 1)
-    for event in range(2):
-        for o in range(3):
-            ax = ORDERS[o][2]
-            hop[o][event].wait_recv()
-            sib[o].append(gsend(o, where_(o, (A, B)[event], ALL, near(ax, 2)), sibling))
-    for o in range(3):
-        absorb(core, o, 2)
-    for o in range(3):
-        sib[o][5].wait_recv()
-        sib[o][6].wait_recv()
-        absorb(other, o, 2)
+    for o in range(3):
+        for c in hop[o]:
+            c.wait_recv()
+        sib[o].append(gsend(o, where_(o, ALL, ALL, near(ORDERS[o][2], 2)), sibling))
 
     expert = lax.rem(dp * 4 + z0, EXPERTS).astype(F32)
-    told = g[0, 2, :, :, :, :, 512:640].reshape(1024, 128).astype(F32)
+    told = g[core, 2, :, :, :, :, 512:640].reshape(1024, 128).astype(F32)
     share_s[...] = jnp.broadcast_to(told[:, 24:25] + told[:, 25:26], (1024, 128))
     turned = told.T
     hit8 = turned[0:8] == expert
@@ -311,49 +306,64 @@
             jnp.sum(chosen_y * p_row[:, cols], axis=1, keepdims=True), (SLOTS, 128)
         )
 
-    def hidden(y, carry):
-        x = jnp.concatenate(
-            [
-                g[h, o, y].reshape(CHUNK, CARRY)[:, : WIDTHS[o]]
-                for h in range(2)
-                for o in range(3)
-            ],
-            axis=1,
-        )
-        xe[pl.ds(pl.multiple_of(y * SLOTS, SLOTS), SLOTS)] = jnp.dot(
-            place[y], x, preferred_element_type=F32
-        ).astype(BF)
-        share_y = share_s[pl.ds(pl.multiple_of(y * CHUNK, CHUNK), CHUNK)]
+    def pick(h):
+        for y in range(4):
+            for o in range(3):
+                x = g[h, o, y].reshape(CHUNK, CARRY)[:, : WIDTHS[o]]
+                r = jnp.dot(place[y], x, preferred_element_type=F32)
+                xe[h, y * SLOTS : (y + 1) * SLOTS, OFFS[o] : OFFS[o] + WIDTHS[o]] = r.astype(BF)
+
+    for o in range(3):
+        absorb(core, o, 2)
+    pick(core)
+    for o in range(3):
+        sib[o][3].wait_recv()
+        absorb(other, o, 2)
+    pick(other)
+    for y in range(4):
+        share_y = share_s[y * CHUNK : (y + 1) * CHUNK]
         hs = silu(acc_g[y].reshape(CHUNK, HID)) * acc_u[y].reshape(CHUNK, HID)
         lhs[y, :, 0:128] = (hs[:, 0:128] * share_y).astype(BF)
         lhs[y, :, 128:HID] = (hs[:, 128:HID] * share_y[:, 0 : HID - 128]).astype(BF)
-        return carry
-
-    lax.fori_loop(0, 4, hidden, 0, unroll=True)
+
+    lhs_over = to_sibling(4, lhs, lhs_in)
+    lhs_over.start()
 
     def expert_hidden(i, carry):
         cols = pl.ds(pl.multiple_of(i * 128, 128), 128)
         w = jnp.concatenate([weg[:, cols], weu[:, cols]], axis=1)
-        r = jnp.dot(xe[...], w, preferred_element_type=F32)
+        rows = jnp.concatenate([xe[0], xe[1]], axis=1)
+        r = jnp.dot(rows, w, preferred_element_type=F32)
         he[:, cols] = (silu(r[:, 0:128]) * r[:, 128:256]).astype(BF)
         return carry
 
     lax.fori_loop(0, HALF // 128, expert_hidden, 0, unroll=True)
 
+    def expert_down(h, at, w):
+        cols = pl.ds(pl.multiple_of(h * HALF_D + at, 128), w)
+        r = jnp.dot(he[...], wed[:, cols], preferred_element_type=F32)
+        return (r * jnp.concatenate([pslot[...]] * (w // 128), axis=1)).astype(BF)
+
+    res_over = []
+    for o in range(3):
+        cols = slice(OFFS[o], OFFS[o] + WIDTHS[o])
+        down = expert_down(other, OFFS[o], WIDTHS[o])
+        res[:, :, cols] = down.reshape(4, SLOTS, WIDTHS[o])
+        cols = pl.ds(OFFS[o], WIDTHS[o])
+        over = to_sibling(5 + o, res.at[:, :, cols], rhs.at[1, :, pl.ds(HID, SLOTS), cols])
+        over.start()
+        res_over.append(over)
+    for o in range(3):
+        cols = slice(OFFS[o], OFFS[o] + WIDTHS[o])
+        down = expert_down(core, OFFS[o], WIDTHS[o])
+        rhs[0, :, HID : HID + SLOTS, cols] = down.reshape(4, SLOTS, WIDTHS[o])
     for copy in again:
         copy.wait()
-
-    by = jnp.concatenate([pslot[...]] * 4, axis=1)
-    for h in range(2):
-        for at, w in ((0, 512), (512, 512), (1024, 512), (1536, 256)):
-            r = jnp.dot(
-                he[...], wed[:, h * HALF_D + at : h * HALF_D + at + w], preferred_element_type=F32
-            )
-            r = (r * by[:, 0:w]).astype(BF)
-            for y in range(4):
-                rhs[h, y, HID : HID + SLOTS, at : at + w] = r[y * SLOTS : (y + 1) * SLOTS]
-
-    s, t, u = (s0, s1, s2), (t0, t1, t2), (u0, u1, u2)
+    for c in across + [lhs_over]:
+        c.wait_recv()
+
+    s = (s0, s1, s2)
+    n_gather = len(pending)
     half_in = (a0, a1, a2)
     full_in = (b0, b1, b2)
     last_in = (c0, c1, c2)
@@ -371,11 +381,12 @@
         pending.append(c)
         return c
 
-    def combine(o, h, to):
+    def combine(o):
         cols = slice(OFFS[o], OFFS[o] + WIDTHS[o])
         for y in range(4):
-            r = jnp.dot(lhs[y], rhs[h, y, :, cols], preferred_element_type=F32)
-            to[y] = r.astype(BF).reshape(4, 4, PAIR, WIDTHS[o])
+            r = jnp.dot(lhs[y], rhs[0, y, :, cols], preferred_element_type=F32)
+            r = r + jnp.dot(lhs_in[y], rhs[1, y, :, cols], preferred_element_type=F32)
+            s[o][y] = r.astype(BF).reshape(4, 4, PAIR, WIDTHS[o])
 
     def at1(o, c, half):
         rest = [half, ALL]
@@ -384,7 +395,7 @@
     def add1(o, c, lo, hi, terms):
         def step(i, carry):
             at = at1(o, c, i)
-            total = s[o][at].astype(F32) + u[o][at].astype(F32)
+            total = s[o][at].astype(F32)
             for term, base in terms:
                 total = total + term[i - base].astype(F32)
             s[o][at] = total.astype(BF)
@@ -392,35 +403,20 @@
 
         lax.fori_loop(lo, hi, step, 0)
 
-    for o in range(3):
-        combine(o, other, t[o])
-    sib = [[], [], []]
-    for k in (2, 1, 3, 0):
-        for o in range(3):
-            at = at1(o, near(ORDERS[o][2], k), ALL)
-            sib[o].append(rsend(t[o].at[at], u[o].at[at], sibling))
-    for o in range(3):
-        combine(o, core, s[o])
-
     stage = [[], [], []]
     for o in range(3):
+        res_over[o].wait_recv()
+        combine(o)
         ax = ORDERS[o][2]
-        c = near(ax, 2)
-        sib[o][0].wait_recv()
-        add1(o, c, 0, 2, [])
-        stage[o].append(rsend(s[o].at[at1(o, c, A)], half_in[o].at[0], peer(ax, 1)))
-        add1(o, c, 2, 4, [])
-        stage[o].append(rsend(s[o].at[at1(o, c, B)], half_in[o].at[1], peer(ax, 3)))
-    for o in range(3):
-        ax = ORDERS[o][2]
-        c = near(ax, 1)
-        sib[o][1].wait_recv()
-        add1(o, c, 2, 4, [])
-        stage[o].append(rsend(s[o].at[at1(o, c, B)], full_in[o].at[0, B], peer(ax, 1)))
-        c = near(ax, 3)
-        sib[o][2].wait_recv()
-        add1(o, c, 0, 2, [])
-        stage[o].append(rsend(s[o].at[at1(o, c, A)], full_in[o].at[1, A], peer(ax, 3)))
+        far = near(ax, 2)
+        stage[o] += [
+            rsend(s[o].at[at1(o, far, A)], half_in[o].at[0], peer(ax, 1)),
+            rsend(s[o].at[at1(o, far, B)], half_in[o].at[1], peer(ax, 3)),
+            rsend(s[o].at[at1(o, near(ax, 1), B)], full_in[o].at[0, B], peer(ax, 1)),
+            rsend(s[o].at[at1(o, near(ax, 3), A)], full_in[o].at[1, A], peer(ax, 3)),
+        ]
+    for c in zc + [swap] + across + [lhs_over] + res_over + pending[:n_gather]:
+        c.wait_send()
     for o in range(3):
         ax = ORDERS[o][2]
         c = near(ax, 1)
@@ -437,7 +433,6 @@
 
     stage2 = []
     for o in range(3):
-        sib[o][3].wait_recv()
         for c in stage[o][2:]:
             c.wait_recv()
         add1(o, own[o][2], 0, 4, [(full_in[o].at[0], 0), (full_in[o].at[1], 0)])
@@ -449,6 +444,8 @@
             ]
         )
 
+    for c in pending[n_gather : n_gather + 18]:
+        c.wait_send()
     stage3 = []
     for o in range(3):
         for c in stage2[o]:
@@ -489,11 +486,8 @@
     both_out[1, :, 0:HALF_D] = jnp.where(first, mine, theirs).astype(BF)
     both_out[1, :, HALF_D:D] = jnp.where(first, theirs, mine).astype(BF)
 
-    for c in zc:
-        c.wait_send()
-    swap.wait_send()
     swap_back.wait_send()
-    for c in pending:
+    for c in pending[n_gather + 18 :]:
         c.wait_send()
 
 
@@ -511,19 +505,19 @@
         V((2, 4, TOK, HALF_D), F32), V((4, PAIR, HALF_D), BF), V((3, PAIR, HALF_D), BF),
         V((2, TOK, HALF_D + 128), F32), V((TOK, HALF_D + 128), F32),
         V((2, 3, 4, 4, 4, PAIR, CARRY), BF),
+        V((2, HID, HALF_D), BF), V((4, SLOTS, HALF_D), BF), V((4, CHUNK, 256), BF),
         V((4, 4, 4, PAIR, HID), F32), V((4, 4, 4, PAIR, HID), F32),
         V((4, SLOTS, CHUNK), BF), V((4 * SLOTS, 128), F32), V((1024, 128), F32),
-        V((4, CHUNK, 256), BF), V((4 * SLOTS, D), BF), V((4 * SLOTS, HALF), BF),
+        V((4, CHUNK, 256), BF), V((2, 4 * SLOTS, HALF_D), BF), V((4 * SLOTS, HALF), BF),
     ]
-    for _ in range(3):
-        scratch += [V((4, 4, 4, PAIR, w), BF) for w in WIDTHS]
+    scratch += [V((4, 4, 4, PAIR, w), BF) for w in WIDTHS]
     scratch += [V((2, 2, 4, PAIR, w), BF) for w in WIDTHS]
     scratch += [V((2, 4, 4, PAIR, w), BF) for w in WIDTHS]
     scratch += [V((3, 4, PAIR, w), BF) for w in WIDTHS]
     scratch += [V((3, PAIR, w), BF) for w in WIDTHS]
     scratch += [V((2, TOK, HALF_D), F32), V((TOK, HALF_D), F32)]
     scratch += [
-        dma((8,)), dma((6,)), dma((3,)), dma((3,)), dma((4,)),
+        dma((8,)), dma((4,)), dma((8,)), dma((8,)), dma((3,)), dma((3,)), dma((4,)),
         dma((N_AG,)), dma((N_AG,)), dma((N_RS,)), dma((N_RS,)),
     ]
     both = pl.pallas_call(

time: 82.4 us -> 80.6 us (0.978)
  Pallas kernels: 80 us -> 78.2 us
    pallas_call x1, Pallas kernels: 80 us -> 78.2 us  [on_device(): pl.pallas_call(kernel, out_shape=jax.ShapeDtypeStruct((2, TOK, D), BF), i...]
where the time goes in v3:
time: 80.6 us; the launch traced here: 80.4 us
  Pallas kernels  78.2 us (97%)
  local copies, waits for them, and re-layouts  1.49 us (2%)
    pallas_call x1, Pallas kernels, on_device(): pl.pallas_call(kernel, out_shape=jax.ShapeDtypeStruct((2, TOK, D), BF), i...  78.2 us

profile of v3, /device:TPU:1, one launch (start us, length us, event | category | flops | bytes accessed | tf_op | source)
XLA Modules:
  0.0 80.4 jit_solution(11902122489864177263)
XLA Ops:
  0.6 78.2 %shard_map.140 = bf16[2,8,3584]{2,1,0:T(8,128)(2,1)} custom-call(bf16[32,896]{1,0:T(8,128)(2,1)} %heads.1, bf16[896,3584]{1,0:T(8,128)(2,1)} %out_w.1, bf16[8,3584]{1,0:T(8,128)(2,1)} %residual.1, bf16[3584]{0:T(1024)(128)(2,1)} %gain.1, bf16[3584]{0:T(1024)(128)(2,1)} %sgate.1, bf16[160,3584]{1,0:T(8,128)(2,1)} %bitcast.6, bf16[160,3584]{1,0:T(8,128)(2,1)} %bitcast.7, ...), custom_call_target="tpu_custom_call" | custom-call | tf_op jit(solution)/shard_map/pallas_call | solution.py:523
  78.9 1.5 %slice_bitcast_fusion = (bf16[8,3584]{1,0:T(8,128)(2,1)}, bf16[8,3584]{1,0:T(8,128)(2,1)}) fusion(bf16[2,8,3584]{2,1,0:T(8,128)(2,1)} %shard_map.140), kind=kLoop, calls=%fused_computation | loop fusion | bytes 229376 | tf_op jit(solution)/shard_map/squeeze | solution.py:537

commit v4 on v3

--- a/solution.py
+++ b/solution.py
@@ -100,7 +100,7 @@
     pl.semaphore_wait(barrier, 10)
 
     zc = []
-    for k in range(1, 4):
+    for k in (2, 1, 3):
         c = pltpu.make_async_remote_copy(
             src_ref=sbuf.at[near(2, k)], dst_ref=rz.at[k - 1],
             send_sem=zs_sem.at[k - 1], recv_sem=zr_sem.at[k - 1],
@@ -205,7 +205,7 @@
     ALL, A, B = pl.ds(0, 4), pl.ds(0, 2), pl.ds(2, 2)
     own = [[pos[axis] for axis in ORDERS[o]] for o in range(3)]
 
-    got = [[gsend(o, pos, peer(ORDERS[o][0], k)) for k in (1, 3, 2)] for o in range(3)]
+    got = [[gsend(o, pos, peer(ORDERS[o][0], k)) for k in (2, 1, 3)] for o in range(3)]
     for load in loads[4:]:
         load.start()
     acc_g[...] = jnp.zeros((4, 4, 4, PAIR, HID), F32)
@@ -227,7 +227,7 @@
         for c in got[o]:
             c.wait_recv()
         mine_at = where_(o, ALL, own[o][1], own[o][2])
-        hop.append([gsend(o, mine_at, peer(ORDERS[o][1], k)) for k in (1, 3, 2)])
+        hop.append([gsend(o, mine_at, peer(ORDERS[o][1], k)) for k in (2, 1, 3)])
     for load in loads[4:]:
         load.wait()
     for copy in again + across:
@@ -431,18 +431,25 @@
     def at2(o, c):
         return tuple(where_(o, ALL, c, own[o][2]))
 
+    def line_sum(o, c):
+        rest = [axis for axis in range(3) if axis != ORDERS[o][2]]
+        at = (c,) if rest[0] == ORDERS[o][1] else (ALL, c)
+        total = s[o][at2(o, c)].astype(F32)
+        for side in range(2):
+            total = total + full_in[o][(side,) + at].astype(F32)
+        return total
+
     stage2 = []
     for o in range(3):
         for c in stage[o][2:]:
             c.wait_recv()
-        add1(o, own[o][2], 0, 4, [(full_in[o].at[0], 0), (full_in[o].at[1], 0)])
         ax = ORDERS[o][1]
-        stage2.append(
-            [
-                rsend(s[o].at[at2(o, near(ax, k))], last_in[o].at[k - 1], peer(ax, k))
-                for k in (1, 3, 2)
-            ]
-        )
+        sent = []
+        for k in (2, 1, 3):
+            at = at2(o, near(ax, k))
+            s[o][at] = line_sum(o, near(ax, k)).astype(BF)
+            sent.append(rsend(s[o].at[at], last_in[o].at[k - 1], peer(ax, k)))
+        stage2.append(sent)
 
     for c in pending[n_gather : n_gather + 18]:
         c.wait_send()
@@ -451,7 +458,7 @@
         for c in stage2[o]:
             c.wait_recv()
         at = at2(o, own[o][1])
-        total = s[o][at].astype(F32)
+        total = line_sum(o, own[o][1])
         for k in range(3):
             total = total + last_in[o][k].astype(F32)
         s[o][at] = total.astype(BF)
@@ -463,13 +470,14 @@
                     one_in[o].at[k - 1],
                     peer(ax, k),
                 )
-                for k in (1, 2, 3)
+                for k in (2, 1, 3)
             ]
         )
     for o in range(3):
         total = s[o][pos].astype(F32)
+        for c in stage3[o]:
+            c.wait_recv()
         for k in range(3):
-            stage3[o][k].wait_recv()
             total = total + one_in[o][k].astype(F32)
         cols = pl.ds(OFFS[o], WIDTHS[o])
         fin[0, :, cols] = total[0:TOK]

time: 80.6 us -> 79.6 us (0.988)
  Pallas kernels: 78.2 us -> 77.2 us
    pallas_call x1, Pallas kernels: 78.2 us -> 77.2 us  [on_device(): pl.pallas_call(kernel, out_shape=jax.ShapeDtypeStruct((2, TOK, D), BF), i...]
where the time goes in v4:
time: 79.6 us; the launch traced here: 79.4 us
  Pallas kernels  77.2 us (97%)
  local copies, waits for them, and re-layouts  1.49 us (2%)
    pallas_call x1, Pallas kernels, on_device(): pl.pallas_call(kernel, out_shape=jax.ShapeDtypeStruct((2, TOK, D), BF), i...  77.2 us

profile of v4, /device:TPU:1, one launch (start us, length us, event | category | flops | bytes accessed | tf_op | source)
XLA Modules:
  0.0 79.4 jit_solution(11492722219134809056)
XLA Ops:
  0.6 77.2 %shard_map.140 = bf16[2,8,3584]{2,1,0:T(8,128)(2,1)} custom-call(bf16[32,896]{1,0:T(8,128)(2,1)} %heads.1, bf16[896,3584]{1,0:T(8,128)(2,1)} %out_w.1, bf16[8,3584]{1,0:T(8,128)(2,1)} %residual.1, bf16[3584]{0:T(1024)(128)(2,1)} %gain.1, bf16[3584]{0:T(1024)(128)(2,1)} %sgate.1, bf16[160,3584]{1,0:T(8,128)(2,1)} %bitcast.6, bf16[160,3584]{1,0:T(8,128)(2,1)} %bitcast.7, ...), custom_call_target="tpu_custom_call" | custom-call | tf_op jit(solution)/shard_map/pallas_call | solution.py:531
  77.9 1.5 %slice_bitcast_fusion = (bf16[8,3584]{1,0:T(8,128)(2,1)}, bf16[8,3584]{1,0:T(8,128)(2,1)}) fusion(bf16[2,8,3584]{2,1,0:T(8,128)(2,1)} %shard_map.140), kind=kLoop, calls=%fused_computation | loop fusion | bytes 229376 | tf_op jit(solution)/shard_map/squeeze | solution.py:545

commit v5 on v4

--- a/solution.py
+++ b/solution.py
@@ -75,8 +75,8 @@
         load.start()
 
     barrier = pltpu.get_barrier_semaphore()
-    for axis in range(3):
-        for k in range(1, 4):
+    for k in (2, 1, 3):
+        for axis in (2, 1, 0):
             pl.semaphore_signal(barrier, inc=1, device_id=peer(axis, k), device_id_type=MESH)
     pl.semaphore_signal(barrier, inc=1, device_id=sibling, device_id_type=MESH)
 
@@ -126,6 +126,7 @@
         c.wait_recv()
 
     square = jnp.zeros((TOK, 1), F32)
+    logit = jnp.zeros((TOK, 1), F32)
     mids = []
     for h in range(2):
         cols = slice(h * HALF_D, (h + 1) * HALF_D)
@@ -137,14 +138,14 @@
         midf = mid.astype(F32)
         mids.append(midf)
         square = square + jnp.sum(midf * midf, axis=1, keepdims=True)
+        toward = gain[cols].astype(F32).reshape(1, HALF_D) * sgate[cols].astype(F32).reshape(1, HALF_D)
+        logit = logit + jnp.sum(midf * toward, axis=1, keepdims=True)
     scale = lax.rsqrt(square * (1.0 / D) + 1e-06)
-    logit = jnp.zeros((TOK, 1), F32)
     for h in range(2):
         cols = slice(h * HALF_D, (h + 1) * HALF_D)
         normed = (mids[h] * scale * gain[cols].astype(F32).reshape(1, HALF_D)).astype(BF).astype(F32)
         nx[h, :, 0:HALF_D] = normed
-        logit = logit + jnp.sum(normed * sgate[cols].astype(F32).reshape(1, HALF_D), axis=1, keepdims=True)
-    share = 1.0 / (1.0 + jnp.exp(-logit))
+    share = 1.0 / (1.0 + jnp.exp(-logit * scale))
 
     share_high = share.astype(BF).astype(F32)
     facts = jnp.where(lane == 24, share_high, facts)
@@ -205,7 +206,10 @@
     ALL, A, B = pl.ds(0, 4), pl.ds(0, 2), pl.ds(2, 2)
     own = [[pos[axis] for axis in ORDERS[o]] for o in range(3)]
 
-    got = [[gsend(o, pos, peer(ORDERS[o][0], k)) for k in (2, 1, 3)] for o in range(3)]
+    got = [[], [], []]
+    for k in (2, 1, 3):
+        for o in range(3):
+            got[o].append(gsend(o, pos, peer(ORDERS[o][0], k)))
     for load in loads[4:]:
         load.start()
     acc_g[...] = jnp.zeros((4, 4, 4, PAIR, HID), F32)

time: 79.6 us -> 79.5 us (level)
  no operation moved by 1% of the time
where the time goes in v5:
time: 79.5 us; the launch traced here: 79.3 us
  Pallas kernels  77.2 us (97%)
  local copies, waits for them, and re-layouts  1.49 us (2%)
    pallas_call x1, Pallas kernels, on_device(): pl.pallas_call(kernel, out_shape=jax.ShapeDtypeStruct((2, TOK, D), BF), i...  77.2 us

profile of v5, /device:TPU:1, one launch (start us, length us, event | category | flops | bytes accessed | tf_op | source)
XLA Modules:
  0.0 79.3 jit_solution(17348207089555481842)
XLA Ops:
  0.6 77.2 %shard_map.140 = bf16[2,8,3584]{2,1,0:T(8,128)(2,1)} custom-call(bf16[32,896]{1,0:T(8,128)(2,1)} %heads.1, bf16[896,3584]{1,0:T(8,128)(2,1)} %out_w.1, bf16[8,3584]{1,0:T(8,128)(2,1)} %residual.1, bf16[3584]{0:T(1024)(128)(2,1)} %gain.1, bf16[3584]{0:T(1024)(128)(2,1)} %sgate.1, bf16[160,3584]{1,0:T(8,128)(2,1)} %bitcast.6, bf16[160,3584]{1,0:T(8,128)(2,1)} %bitcast.7, ...), custom_call_target="tpu_custom_call" | custom-call | tf_op jit(solution)/shard_map/pallas_call | solution.py:535
  77.8 1.5 %slice_bitcast_fusion = (bf16[8,3584]{1,0:T(8,128)(2,1)}, bf16[8,3584]{1,0:T(8,128)(2,1)}) fusion(bf16[2,8,3584]{2,1,0:T(8,128)(2,1)} %shard_map.140), kind=kLoop, calls=%fused_computation | loop fusion | bytes 229376 | tf_op jit(solution)/shard_map/squeeze | solution.py:549
